TPU v7x, 512 devices: a whole 4x4x16 slice. The times are simulated.
512 devices in a mesh: row: 32 (over y, x, core), col: 16 (over z).
Axes of the slice: x: 4, y: 4, z: 16, core: 2. Of those that a mesh axis runs over, the one named last changes fastest.
Arguments:
- left_factors: bfloat16 [2, 32, 2, 16, 512, 128], P(None, 'row', None, 'col'), may hold values from -6 to 6
- right_factors: bfloat16 [2, 32, 2, 16, 512, 128], P(None, 'row', None, 'col'), may hold values from -0.5 to 0.5
- ranks: int32 [2, 32, 2, 16], P(None, 'row', None, 'col'), may hold values from 32 to 128, as said below
- pivot_inverses: bfloat16 [2, 512, 512], replicated, may hold values from -0.0048828125 to 0.0048828125
Outputs:
- factored: bfloat16 [2, 32, 2, 16, 512, 512], P(None, 'row', None, 'col')
Inputs may be any that keep to these rules, and one draw needn't show every extreme that they name: `ranks`: every rank is a multiple of 16.
All inputs are finite; a program needn't handle non-finite values.
Results may differ from a plain program's by a relative error of at most 0.0054.
Values may be sent and summed in bfloat16 or wider, within the bound.
No kernel may reach another device: no remote copies, remote signals or barrier semaphores. Data moves between devices by JAX's collectives and lax.ppermute only.
A program may use at most 64 MiB of HBM per device.

v0:
```python
import jax
import jax.numpy as jnp
from jax import lax
from jax.sharding import PartitionSpec as P


def broadcast(shard, axis, root):
    mine = lax.axis_index(axis) == root
    return lax.psum(jnp.where(mine, shard, jnp.zeros_like(shard)), axis)


def transform(inverse, factors):
    return jnp.einsum(
        "kn,...kr->...nr", inverse, factors, preferred_element_type=jnp.float32
    ).astype(jnp.bfloat16)


def per_device(left_factors, right_factors, ranks, pivot_inverses):
    rows_local = left_factors.shape[0]
    cols_local = left_factors.shape[2]
    tile_size = left_factors.shape[4]
    factor_cols = left_factors.shape[5]
    n_rows = lax.axis_size("row")
    n_cols = lax.axis_size("col")
    row_ids = jnp.arange(rows_local, dtype=jnp.int32) * n_rows + lax.axis_index("row")
    col_ids = jnp.arange(cols_local, dtype=jnp.int32) * n_cols + lax.axis_index("col")
    shape_four = (rows_local, cols_local, tile_size, factor_cols)
    rank_grid = ranks.reshape(rows_local, cols_local)
    rank_keep = (
        jnp.arange(factor_cols, dtype=jnp.int32)[None, None, None, :] < rank_grid[:, :, None, None]
    )
    left_tiles = jnp.where(rank_keep, left_factors.reshape(shape_four), 0.0)
    right_tiles = jnp.where(rank_keep, right_factors.reshape(shape_four), 0.0)
    inverse_one = pivot_inverses[0]
    inverse_two = pivot_inverses[1]
    payload = transform(inverse_one, right_tiles[:, 0])
    got_left, got_right = (broadcast(left_tiles[:, 0], "col", 0), broadcast(payload, "col", 0))
    up_left, up_right = (broadcast(left_tiles[0], "row", 0), broadcast(right_tiles[0], "row", 0))
    mask_one = ((row_ids[:, None] > 0) & (col_ids[None, :] > 0))[:, :, None, None]
    middle_one = jnp.einsum("anr,bns->abrs", got_right, up_left, preferred_element_type=jnp.float32)
    middle_one = jnp.where(mask_one, middle_one, 0.0).astype(jnp.bfloat16)
    update_one = jnp.einsum(
        "anr,abrs->abns", got_left, middle_one, preferred_element_type=jnp.float32
    ).astype(jnp.bfloat16)
    own_right = right_tiles[:, 0]
    pivot_raw = up_right[0]
    fresh = transform(inverse_two, own_right)
    pivot = transform(inverse_two, pivot_raw)
    right_send = jnp.concatenate([fresh, jnp.broadcast_to(pivot[None], fresh.shape)], axis=-1)
    left_send = jnp.concatenate([left_tiles[:, 0], -update_one[:, 0]], axis=-1)
    second_left, second_right = (broadcast(left_send, "col", 1), broadcast(right_send, "col", 1))
    upper_left, upper_right = (
        broadcast(jnp.concatenate([left_tiles[0], -update_one[0]], axis=-1), "row", 1),
        broadcast(jnp.concatenate([right_tiles[0], up_right], axis=-1), "row", 1),
    )
    mask_two = ((row_ids[:, None] > 1) & (col_ids[None, :] > 1))[:, :, None, None]
    middle_two = jnp.einsum(
        "anr,bns->abrs", second_right, upper_left, preferred_element_type=jnp.float32
    )
    middle_two = jnp.where(mask_two, middle_two, 0.0).astype(jnp.bfloat16)
    update_two = jnp.einsum(
        "anr,abrs->abns", second_left, middle_two, preferred_element_type=jnp.float32
    ).astype(jnp.bfloat16)
    is_first = ((col_ids[None, :] == 0) & (row_ids[:, None] > 0))[:, :, None, None]
    is_second = ((col_ids[None, :] == 1) & (row_ids[:, None] > 1))[:, :, None, None]
    fresh_block = second_right[:, None, :, :factor_cols]
    pivot_block = second_right[:, None, :, factor_cols:]
    first_block = jnp.where(
        is_first, got_right[:, None], jnp.where(is_second, fresh_block, right_tiles)
    )
    second_block = jnp.where(is_second, pivot_block, up_right[None])
    upper_block = jnp.broadcast_to(
        upper_right[None], (rows_local, cols_local, tile_size, 2 * factor_cols)
    )
    all_left = jnp.concatenate([left_tiles, -update_one, -update_two], axis=-1)
    all_right = jnp.concatenate([first_block, second_block, upper_block], axis=-1)
    dense = jnp.einsum(
        "abnr,abmr->abnm", all_left, all_right, preferred_element_type=jnp.float32
    ).astype(jnp.bfloat16)
    return dense.reshape(rows_local, 1, cols_local, 1, tile_size, tile_size)


def solution(mesh):
    in_specs = (
        P(None, "row", None, "col", None, None),
        P(None, "row", None, "col", None, None),
        P(None, "row", None, "col"),
        P(),
    )
    out_specs = P(None, "row", None, "col", None, None)
    return jax.shard_map(
        per_device, mesh=mesh, in_specs=in_specs, out_specs=out_specs, check_vma=False
    )
```

profile of v0, /device:TPU:2, one launch (start us, length us, event | category | flops | bytes accessed | tf_op | source)
XLA Modules:
  0.0 582.7 jit_solution(2579741472013417850)
XLA Ops:
  6.5 0.8 copy.5
  7.4 1.2 copy.6
  8.6 1.2 copy.8
  10.0 0.7 broadcast_select_fusion.2
  10.8 0.8 broadcast_select_fusion.1
  11.7 1.0 fusion.23
  12.8 0.3 fusion.20
  13.4 136.7 %all-reduce.11.cloned.1.call-done = (bf16[2,512,128]{1,2,0:T(8,128)(2,1)}, bf16[2,512,128]{1,2,0:T(8,128)(2,1)}) async-done(((bf16[2,512,128]{1,2,0:T(8,128)(2,1)}, bf16[2,512,128]{1,2,0:T(8,128)(2,1)}), (bf16[2,512,128]{1,2,0:T(8,128)(2,1)}, bf16[2,512,128]{1,2,0:T(8,128)(2,1)})) %all-reduce.11.cloned.1.call-update) | async-done | bytes 524304 | tf_op jit(solution)/shard_map/psum | solution.py:9
  150.1 1.8 maximum_select_fusion.3
  151.9 137.8 %all-reduce.15.cloned.1.call-done = (bf16[2,512,128]{1,2,0:T(8,128)(2,1)}, bf16[2,512,128]{1,2,0:T(8,128)(2,1)}) async-done(((bf16[2,512,128]{1,2,0:T(8,128)(2,1)}, bf16[2,512,128]{1,2,0:T(8,128)(2,1)}), (bf16[2,512,128]{1,2,0:T(8,128)(2,1)}, bf16[2,512,128]{1,2,0:T(8,128)(2,1)})) %all-reduce.15.cloned.1.call-update) | async-done | bytes 524304 | tf_op jit(solution)/shard_map/psum | solution.py:9
  289.7 1.3 fusion.24
  291.0 1.3 fusion.50
  292.3 0.9 maximum_select_fusion
  293.3 1.3 fusion.25
  294.6 0.9 maximum_select_fusion.1
  295.5 0.9 maximum_select_fusion.2
  296.4 1.0 copy.12
  297.7 1.0 copy.13
  298.7 126.5 %all-reduce.9.cloned.1.call-done = (bf16[2,512,256]{1,2,0:T(8,128)(2,1)}, bf16[2,512,256]{1,2,0:T(8,128)(2,1)}) async-done(((bf16[2,512,256]{1,2,0:T(8,128)(2,1)}, bf16[2,512,256]{1,2,0:T(8,128)(2,1)}), (bf16[2,512,256]{1,2,0:T(8,128)(2,1)}, bf16[2,512,256]{1,2,0:T(8,128)(2,1)})) %all-reduce.9.cloned.1.call-update) | async-done | bytes 1048592 | tf_op jit(solution)/shard_map/psum | solution.py:9
  425.2 1.2 copy.14
  426.4 140.6 %all-reduce.13.cloned.1.call-done = (bf16[2,512,256]{1,2,0:T(8,128)(2,1)}, bf16[2,512,256]{1,2,0:T(8,128)(2,1)}) async-done(((bf16[2,512,256]{1,2,0:T(8,128)(2,1)}, bf16[2,512,256]{1,2,0:T(8,128)(2,1)}), (bf16[2,512,256]{1,2,0:T(8,128)(2,1)}, bf16[2,512,256]{1,2,0:T(8,128)(2,1)})) %all-reduce.13.cloned.1.call-update) | async-done | bytes 1048592 | tf_op jit(solution)/shard_map/psum | solution.py:9
  567.0 1.1 fusion.49
  569.2 3.1 fusion.16
  572.3 3.8 convert_bitcast_fusion
  (39 shorter events, 2.0 us)
Async XLA Ops:
  6.5 143.5 %all-reduce.11.cloned.1.call-start = ((), (), s32[]{:S(2)}) async-start(), calls=%async_computation.1 | async-start | bytes 1048576 | tf_op jit(solution)/shard_map/psum | solution.py:9
  9.9 1.8 copy-start.5
  11.6 278.1 %all-reduce.15.cloned.1.call-start = ((), (), s32[]{:S(2)}) async-start(), calls=%async_computation.3 | async-start | bytes 1048576 | tf_op jit(solution)/shard_map/psum | solution.py:9
  12.7 412.5 %all-reduce.9.cloned.1.call-start = ((), (), s32[]{:S(2)}) async-start(), calls=%async_computation | async-start | bytes 2097152 | tf_op jit(solution)/shard_map/psum | solution.py:9
  291.0 2.3 copy-start.1
  293.2 273.8 %all-reduce.13.cloned.1.call-start = ((), (), s32[]{:S(2)}) async-start(), calls=%async_computation.2 | async-start | bytes 2097152 | tf_op jit(solution)/shard_map/psum | solution.py:9
  296.4 271.7 %copy-start = (bf16[2,512,128]{1,2,0:T(8,128)(2,1)S(1)}, bf16[2,512,128]{1,2,0:T(8,128)(2,1)}, u32[]{:S(2)}) copy-start(bf16[2,512,128]{1,2,0:T(8,128)(2,1)} %get-tuple-element.12) | copy-start | bytes 786436
  568.1 1.0 copy-start.2
  569.2 3.2 copy-start.3
  569.2 3.2 copy-start.4
Sparse Core Ops, SparseCore 0:
  11.8 138.2 all-reduce.10
  152.5 137.1 all-reduce.14
  293.4 131.7 all-reduce.8
  427.5 139.4 all-reduce.12
where the time goes:
time: 583 us
  waiting for transfers between devices  542 us (93%)
  between operations  13.3 us (2%)
  matrix products  12.1 us (2%)
  local copies, waits for them, and re-layouts  8.74 us (1%)
  other arithmetic  6.74 us (1%)
    psum x4, waiting for transfers between devices, broadcast(): return lax.psum(jnp.where(mine, shard, jnp.zeros_like(shard)), axis)  542 us
  transfers between devices with their start and end apart: 4, of which 4 were waited for; matrix products, arithmetic and copies ran while one was open for 2% of the time, Pallas kernels for 0%

commit v1 on v0

v1 whole, which is shorter than its diff:
```python
import jax
import jax.numpy as jnp
from jax import lax
from jax.sharding import PartitionSpec as P

AG_ROWS = 104
TREE_ROWS = 384
N_COL = 16
N_ROW = 32


def transform(inverse, factors):
    return jnp.einsum(
        "kn,...kr->...nr", inverse, factors, preferred_element_type=jnp.float32
    ).astype(jnp.bfloat16)


def pick(conditions, values):
    out = values[-1]
    for condition, value in zip(reversed(conditions), reversed(values[:-1])):
        out = jnp.where(condition, value, out)
    return out


def column_pieces(panel):
    q = lax.axis_index("col")
    tree = panel[:TREE_ROWS]
    pieces = panel[TREE_ROWS:].reshape(N_COL, AG_ROWS, 128)

    def group(a):
        members = [(4 * a - 1 + m) % N_COL for m in range(4)]
        return jnp.concatenate([tree] + [pieces[m] for m in members], axis=0)

    groups = [group(a) for a in range(4)]
    near = lax.ppermute(jnp.where(q == 0, groups[1], groups[3]), "col", [(0, 4), (1, 13)])
    back = lax.ppermute(jnp.where(q == 0, groups[3], groups[1]), "col", [(0, 12), (1, 5)])
    far = lax.ppermute(groups[2], "col", [(0, 8), (1, 9)])
    return groups[0], near, back, far


def spread(own, near, back, far):
    q = lax.axis_index("col")
    head = pick(
        [q < 2, (q == 4) | (q == 13), (q == 12) | (q == 5)], [own, near, back, far]
    )
    tree = head[:TREE_ROWS]
    part = [head[TREE_ROWS + AG_ROWS * m : TREE_ROWS + AG_ROWS * (m + 1)] for m in range(4)]
    even = q % 4 == 0

    def message(first, second):
        return jnp.concatenate([tree, jnp.where(even, part[first], part[second])], axis=0)

    starts = range(0, N_COL, 4)
    one = lax.ppermute(
        message(2, 1), "col", [(s, s + 1) for s in starts] + [(s + 1, s) for s in starts]
    )
    two = lax.ppermute(
        message(3, 0),
        "col",
        [(s, s + 2) for s in starts] + [(s + 1, (s - 1) % N_COL) for s in starts],
    )
    three = lax.ppermute(
        message(0, 3),
        "col",
        [(s, (s - 1) % N_COL) for s in starts] + [(s + 1, s + 2) for s in starts],
    )
    kept = message(1, 2)
    which = q % 4
    order = [which == 0, which == 1, which == 2]
    first = pick(order, [kept, one, two, three])
    second = pick(order, [one, kept, three, two])
    return first, second


def per_device(left_factors, right_factors, ranks, pivot_inverses):
    shape_four = (2, 2, 512, 128)
    p = lax.axis_index("row")
    q = lax.axis_index("col")
    row_ids = jnp.arange(2, dtype=jnp.int32) * N_ROW + p
    col_ids = jnp.arange(2, dtype=jnp.int32) * N_COL + q
    rank_grid = ranks.reshape(2, 2)
    rank_keep = jnp.arange(128, dtype=jnp.int32)[None, None, None, :] < rank_grid[:, :, None, None]
    left_tiles = jnp.where(rank_keep, left_factors.reshape(shape_four), 0.0)
    right_tiles = jnp.where(rank_keep, right_factors.reshape(shape_four), 0.0)
    inverse_one = pivot_inverses[0]
    inverse_two = pivot_inverses[1]

    panel = jnp.concatenate([left_tiles[:, 0], right_tiles[:, 0]], axis=0).reshape(2048, 128)
    own, near, back, far = column_pieces(panel)

    top = jnp.concatenate([left_tiles[0], right_tiles[0]], axis=0).reshape(4, N_ROW, 16, 128)
    top = top.transpose(1, 0, 2, 3)
    scattered = lax.all_to_all(top, "row", 0, 0, tiled=True)[:2]

    first, second = spread(own, near, back, far)
    corner = jnp.where(q == 0, scattered[1], scattered[0])
    corner = jnp.concatenate([corner[0], corner[2]], axis=0)

    rows_all = lax.all_gather(scattered.reshape(128, 128), "row").reshape(N_ROW, 2, 4, 16, 128)
    rows_all = rows_all.transpose(1, 2, 0, 3, 4).reshape(2, 2, 2, 512, 128)
    up_left, up_right = rows_all[0, 0], rows_all[0, 1]
    low_left, low_right = rows_all[1, 0], rows_all[1, 1]

    gathered = lax.all_gather(
        jnp.concatenate([first[TREE_ROWS:], second[TREE_ROWS:], corner], axis=0), "col"
    )
    corner = jnp.concatenate([gathered[0, 2 * AG_ROWS :], gathered[1, 2 * AG_ROWS :]], axis=0)
    corner = lax.all_to_all(
        jnp.broadcast_to(corner[None], (N_ROW, 64, 128)), "row", 0, 0, tiled=True
    )
    corner = corner.reshape(N_ROW, 4, 16, 128).transpose(1, 0, 2, 3).reshape(4, 512, 128)
    left_ten, right_ten, left_one, right_one = corner[0], corner[1], corner[2], corner[3]

    def assemble(tree, pieces):
        return jnp.concatenate(
            [tree[:TREE_ROWS], pieces.reshape(N_COL * AG_ROWS, 128)], axis=0
        ).reshape(2, 2, 512, 128)

    panel_one = assemble(first, gathered[:, :AG_ROWS])
    panel_two = assemble(second, gathered[:, AG_ROWS : 2 * AG_ROWS])
    got_left, col_left = panel_one[0], panel_two[0]
    got_right = transform(inverse_one, panel_one[1])
    fresh = transform(inverse_two, panel_two[1])
    pivot = transform(inverse_two, right_one)
    lower_ten = transform(inverse_one, right_ten)

    def middle(lower, upper, form, keep):
        product = jnp.einsum(form, lower, upper, preferred_element_type=jnp.float32)
        return jnp.where(keep, product, 0.0).astype(jnp.bfloat16)

    def apply(left, inner, form):
        return jnp.einsum(form, left, inner, preferred_element_type=jnp.float32).astype(
            jnp.bfloat16
        )

    mask_one = ((row_ids[:, None] > 0) & (col_ids[None, :] > 0))[:, :, None, None]
    middle_one = middle(got_right, up_left, "anr,bns->abrs", mask_one)
    update_one = apply(got_left, middle_one, "anr,abrs->abns")
    middle_col = middle(got_right, left_one, "anr,ns->ars", (row_ids > 0)[:, None, None])
    update_col = apply(got_left, middle_col, "anr,ars->ans")
    middle_row = middle(lower_ten, up_left, "nr,bns->brs", (col_ids > 0)[:, None, None])
    update_row = apply(left_ten, middle_row, "nr,brs->bns")

    second_left = jnp.concatenate([col_left, -update_col], axis=-1)
    second_right = jnp.concatenate([fresh, jnp.broadcast_to(pivot[None], fresh.shape)], axis=-1)
    upper_left = jnp.concatenate([low_left, -update_row], axis=-1)
    upper_right = jnp.concatenate([low_right, up_right], axis=-1)
    mask_two = ((row_ids[:, None] > 1) & (col_ids[None, :] > 1))[:, :, None, None]
    middle_two = middle(second_right, upper_left, "anr,bns->abrs", mask_two)
    update_two = apply(second_left, middle_two, "anr,abrs->abns")

    is_first = ((col_ids[None, :] == 0) & (row_ids[:, None] > 0))[:, :, None, None]
    is_second = ((col_ids[None, :] == 1) & (row_ids[:, None] > 1))[:, :, None, None]
    first_block = jnp.where(
        is_first, got_right[:, None], jnp.where(is_second, fresh[:, None], right_tiles)
    )
    second_block = jnp.where(is_second, pivot[None, None], up_right[None])
    upper_block = jnp.broadcast_to(upper_right[None], (2, 2, 512, 256))
    all_left = jnp.concatenate([left_tiles, -update_one, -update_two], axis=-1)
    all_right = jnp.concatenate([first_block, second_block, upper_block], axis=-1)
    dense = jnp.einsum(
        "abnr,abmr->abnm", all_left, all_right, preferred_element_type=jnp.float32
    ).astype(jnp.bfloat16)
    return dense.reshape(2, 1, 2, 1, 512, 512)


def solution(mesh):
    in_specs = (
        P(None, "row", None, "col", None, None),
        P(None, "row", None, "col", None, None),
        P(None, "row", None, "col"),
        P(),
    )
    out_specs = P(None, "row", None, "col", None, None)
    return jax.shard_map(
        per_device, mesh=mesh, in_specs=in_specs, out_specs=out_specs, check_vma=False
    )
```

time: 583 us -> 147 us (0.25)
  the two profiles are of different devices: /device:TPU:2 before, /device:TPU:1 now
where the time goes in v1:
time: 147 us; the launch traced here: 146 us
  starting transfers between devices  45.8 us (31%)
  blocking collectives  32.4 us (22%)
  waiting for transfers between devices  18.9 us (13%)
  local copies, waits for them, and re-layouts  17.6 us (12%)
  between operations  13.9 us (9%)
  matrix products  12.5 us (9%)
  other arithmetic  5.19 us (4%)
    all_gather x1, blocking collectives, per_device(): lax.all_gather(jnp.concatenate([first[TREE_ROWS:], second[TREE_ROWS:], co...  32.4 us
    all_to_all x1, starting transfers between devices, per_device(): lax.all_to_all(jnp.broadcast_to(corner[None], (N_ROW, 64, 128)), 'row', 0...  15.1 us
    ppermute x1, starting transfers between devices, column_pieces(): lax.ppermute(jnp.where(q == 0, groups[3], groups[1]), 'col', [(0, 12), (1...  10.6 us
    all_to_all x1, starting transfers between devices, per_device(): scattered = lax.all_to_all(top, 'row', 0, 0, tiled=True)[:2]  10.4 us
    all_to_all x1, waiting for transfers between devices, per_device(): lax.all_to_all(jnp.broadcast_to(corner[None], (N_ROW, 64, 128)), 'row', 0...  9.9 us
    ppermute x1, waiting for transfers between devices, column_pieces(): lax.ppermute(jnp.where(q == 0, groups[3], groups[1]), 'col', [(0, 12), (1...  7.18 us
    dot_general x4, matrix products, apply(): jnp.einsum(form, left, inner, preferred_element_type=jnp.float32)  5.94 us
    dot_general x1, matrix products, per_device(): jnp.einsum('abnr,abmr->abnm', all_left, all_right, preferred_element_type...  4.03 us
  transfers between devices with their start and end apart: 9, of which 3 were waited for; matrix products, arithmetic and copies ran while one was open for 7% of the time, Pallas kernels for 0%

profile of v1, /device:TPU:1, one launch (start us, length us, event | category | flops | bytes accessed | tf_op | source)
XLA Modules:
  0.0 146.2 jit_solution(3141695106940461882)
XLA Ops:
  7.4 1.2 copy.108
  10.5 10.4 %all-to-all-start = ((bf16[32,4,16,128]{3,2,1,0:T(8,128)(2,1)}), bf16[32,4,16,128]{3,2,1,0:T(8,128)(2,1)S(1)}, u32[]{:S(2)}, u32[]{:S(2)}) async-start(bf16[32,4,16,128]{3,2,1,0:T(8,128)(2,1)} %copy.110), calls=%async_computation | async-start | bytes 1048576 | tf_op jit(solution)/shard_map/all_to_all | solution.py:93
  21.5 10.6 %collective-permute-start.1 = (bf16[800,128]{1,0:T(8,128)(2,1)S(1)}, bf16[800,128]{1,0:T(8,128)(2,1)S(1)}, u32[]{:S(2)}, u32[]{:S(2)}) collective-permute-start(bf16[800,128]{1,0:T(8,128)(2,1)S(1)} %get-tuple-element.25), channel_id=1, source_target_pairs={{0,12},{1,5},{16,28},{17,21},{32,44},{33,37},{48,60},{49,53},{64,7... | collective-permute-start | bytes 614408 | tf_op jit(solution)/shard_map/ppermute | solution.py:36
  32.2 1.3 collective-permute-start
  33.5 3.7 %collective-permute-start.2 = (bf16[800,128]{1,0:T(8,128)(2,1)S(1)}, bf16[800,128]{1,0:T(8,128)(2,1)}, u32[]{:S(2)}, u32[]{:S(2)}) collective-permute-start(bf16[800,128]{1,0:T(8,128)(2,1)S(1)} %get-tuple-element.34), channel_id=1, source_target_pairs={{0,8},{1,9},{16,24},{17,25},{32,40},{33,41},{48,56},{49,57},{64,72... | collective-permute-start | bytes 614408 | tf_op jit(solution)/shard_map/ppermute | solution.py:37
  37.9 7.2 %collective-permute-done.1 = bf16[800,128]{1,0:T(8,128)(2,1)S(1)} collective-permute-done((bf16[800,128]{1,0:T(8,128)(2,1)S(1)}, bf16[800,128]{1,0:T(8,128)(2,1)S(1)}, u32[]{:S(2)}, u32[]{:S(2)}) %collective-permute-start.1) | collective-permute-done | bytes 204832 | tf_op jit(solution)/shard_map/ppermute | solution.py:36
  45.1 1.0 fusion.63
  46.2 1.3 collective-permute-start.4
  47.5 1.9 %collective-permute-start.3 = (bf16[488,128]{1,0:T(8,128)(2,1)S(1)}, bf16[488,128]{1,0:T(8,128)(2,1)S(1)}, u32[]{:S(2)}, u32[]{:S(2)}) collective-permute-start(bf16[488,128]{1,0:T(8,128)(2,1)S(1)} %get-tuple-element.32), channel_id=1, source_target_pairs={{0,1},{4,5},{8,9},{12,13},{1,0},{5,4},{9,8},{13,12},{16,17},{20,21... | collective-permute-start | bytes 374792 | tf_op jit(solution)/shard_map/ppermute | solution.py:54
  49.5 1.3 collective-permute-start.5
  51.4 1.8 %collective-permute-done.3 = bf16[488,128]{1,0:T(8,128)(2,1)S(1)} collective-permute-done((bf16[488,128]{1,0:T(8,128)(2,1)S(1)}, bf16[488,128]{1,0:T(8,128)(2,1)S(1)}, u32[]{:S(2)}, u32[]{:S(2)}) %collective-permute-start.3) | collective-permute-done | bytes 124960 | tf_op jit(solution)/shard_map/ppermute | solution.py:54
  54.0 32.4 %all-gather = bf16[3840,128]{1,0:T(8,128)(2,1)S(1)} all-gather(bf16[240,128]{1,0:T(8,128)(2,1)S(1)} %pad_maximum_fusion.12), channel_id=2, replica_groups=mesh['row'=32,'col'=16] {'col'}, dimensions={0}, use_global_device_ids=true | all-gather | bytes 1044480 | tf_op jit(solution)/shard_map/all_gather | solution.py:104
  87.4 15.1 %all-to-all-start.1 = ((bf16[32,64,128]{2,1,0:T(8,128)(2,1)}), bf16[32,64,128]{2,1,0:T(8,128)(2,1)}, u32[]{:S(2)}, u32[]{:S(2)}) async-start(bf16[32,64,128]{2,1,0:T(8,128)(2,1)} %broadcast_in_dim.150), calls=%async_computation.1 | async-start | bytes 1048576 | tf_op jit(solution)/shard_map/all_to_all | solution.py:108
  103.7 1.0 fusion.21
  105.1 9.9 %all-to-all-done.1 = bf16[32,64,128]{2,1,0:T(8,128)(2,1)} async-done(((bf16[32,64,128]{2,1,0:T(8,128)(2,1)}), bf16[32,64,128]{2,1,0:T(8,128)(2,1)}, u32[]{:S(2)}, u32[]{:S(2)}) %all-to-all-start.1) | async-done | bytes 524320 | tf_op jit(solution)/shard_map/all_to_all | solution.py:108
  115.0 1.8 %fusion.83 = (bf16[1,32,16,128]{3,2,0,1:T(8,128)(2,1)S(1)}, bf16[1,32,16,128]{3,2,0,1:T(8,128)(2,1)S(1)}, bf16[1,32,16,128]{3,2,0,1:T(8,128)(2,1)}, bf16[1,32,16,128]{3,2,0,1:T(8,128)(2,1)S(1)}) fusion(bf16[4,32,16,128]{3,2,0,1:T(8,128)(2,1)} %bitcast.33), kind=kLoop, calls=%fused_computation.131 | loop fusion | bytes 1048576 | tf_op jit(solution)/shard_map/slice | solution.py:112
  118.0 1.1 fusion.25
  119.1 1.4 copy.111
  124.0 2.2 %select_select_fusion = (bf16[2,2,512,128]{2,3,0,1:T(8,128)(2,1)}, bf16[2,2,512,128]{2,3,0,1:T(8,128)(2,1)}) fusion(pred[2,2]{0,1:T(4,128)(4,1)} %copy.123, pred[2,2]{0,1:T(4,128)(4,1)} %copy.122, bf16[2,512,128]{1,2,0:T(8,128)(2,1)} %fusion.21, bf16[2,512,128]{1,2,0:T(8,128)(2,1)S(1)} %bitcast.153, bf16[2,512,128]{1,2,0:T(8,128)(2,1)} %copy.124, ...), kind=kLoop, calls=%fused_computation.59 | loop fusion | flops 1048576 | bytes 2490888 | tf_op jit(solution)/shard_map/jit(_where)/select_n | solution.py:154
  126.2 2.1 %copy.125 = bf16[2,2,512,128]{3,2,1,0:T(8,128)(2,1)} copy(bf16[2,2,512,128]{2,3,0,1:T(8,128)(2,1)} %get-tuple-element.41) | data formatting | bytes 1048576 | tf_op jit(solution)/shard_map/jit(_where)/select_n | solution.py:154
  128.3 2.0 %copy.126 = bf16[2,2,512,128]{3,2,1,0:T(8,128)(2,1)} copy(bf16[2,2,512,128]{2,3,0,1:T(8,128)(2,1)} %get-tuple-element.42) | data formatting | bytes 1048576 | tf_op jit(solution)/shard_map/jit(_where)/select_n | solution.py:157
  130.4 1.2 fusion.24
  132.2 3.0 %fusion.16 = bf16[2,2,512,256]{2,3,1,0:T(8,128)(2,1)} fusion(bf16[2,512,128]{1,2,0:T(8,128)(2,1)} %fusion.24, bf16[2,512,128]{1,2,0:T(8,128)(2,1)} %bitcast.173, bf16[2,512,128]{1,2,0:T(8,128)(2,1)S(1)} %broadcast_in_dim.152, bf16[2,512,128]{1,2,0:T(8,128)(2,1)S(1)} %copy-done.1, bf16[2,512,128]{1,2,0:T(8,128)(2,1)} %fusion.25, ...), kind=kOutput, calls=%fused_computation.14 | convolution fusion | flops 542638080 | bytes 2621444 | tf_op jit(solution)/shard_map/anr,abrs->abns/dot_general | solution.py:132
  135.3 4.0 %convert_bitcast_fusion = bf16[2,1,2,1,512,512]{5,4,3,2,1,0:T(8,128)(2,1)} fusion(bf16[2,2,512,256]{3,2,1,0:T(8,128)(2,1)S(1)} %broadcast_in_dim.162, bf16[2,2,512,128]{3,2,1,0:T(8,128)(2,1)S(1)} %copy-done.4, bf16[2,2,512,128]{3,2,1,0:T(8,128)(2,1)S(1)} %copy-done.3, bf16[2,2,512,256]{2,3,1,0:T(8,128)(2,1)} %fusion.16, ...), kind=kOutput, calls=%fused_computation.11 | convolution fusion | flops 1087373312 | bytes 6291456 | tf_op jit(solution)/shard_map/abnr,abmr->abnm/dot_general | solution.py:161
  (83 shorter events, 13.1 us)
Async XLA Ops:
  6.5 2.5 %copy-start.2 = (bf16[2,1,2,1,512,128]{5,4,3,2,1,0:T(8,128)(2,1)S(1)}, bf16[2,1,2,1,512,128]{5,4,3,2,1,0:T(8,128)(2,1)}, u32[]{:S(2)}) copy-start(bf16[2,1,2,1,512,128]{5,4,3,2,1,0:T(8,128)(2,1)} %param.4) | copy-start | bytes 1572868
  10.5 42.8 %all-to-all-start = ((bf16[32,4,16,128]{3,2,1,0:T(8,128)(2,1)}), bf16[32,4,16,128]{3,2,1,0:T(8,128)(2,1)S(1)}, u32[]{:S(2)}, u32[]{:S(2)}) async-start(bf16[32,4,16,128]{3,2,1,0:T(8,128)(2,1)} %copy.110), calls=%async_computation | async-start | bytes 1048576 | tf_op jit(solution)/shard_map/all_to_all | solution.py:93
  21.0 98.1 %all-gather.3.cloned.1.call-start = ((), (), s32[]{:S(2)}) async-start(), calls=%async_computation.2 | async-start | bytes 1081344 | tf_op jit(solution)/shard_map/all_gather | solution.py:99
  21.5 23.6 %collective-permute-start.1 = (bf16[800,128]{1,0:T(8,128)(2,1)S(1)}, bf16[800,128]{1,0:T(8,128)(2,1)S(1)}, u32[]{:S(2)}, u32[]{:S(2)}) collective-permute-start(bf16[800,128]{1,0:T(8,128)(2,1)S(1)} %get-tuple-element.25), channel_id=1, source_target_pairs={{0,12},{1,5},{16,28},{17,21},{32,44},{33,37},{48,60},{49,53},{64,7... | collective-permute-start | bytes 614408 | tf_op jit(solution)/shard_map/ppermute | solution.py:36
  32.2 12.9 %collective-permute-start = (bf16[800,128]{1,0:T(8,128)(2,1)S(1)}, bf16[800,128]{1,0:T(8,128)(2,1)S(1)}, u32[]{:S(2)}, u32[]{:S(2)}) collective-permute-start(bf16[800,128]{1,0:T(8,128)(2,1)S(1)} %get-tuple-element.26), channel_id=1, source_target_pairs={{0,4},{1,13},{16,20},{17,29},{32,36},{33,45},{48,52},{49,61},{64,6... | collective-permute-start | bytes 614408 | tf_op jit(solution)/shard_map/ppermute | solution.py:35
  33.5 11.6 %collective-permute-start.2 = (bf16[800,128]{1,0:T(8,128)(2,1)S(1)}, bf16[800,128]{1,0:T(8,128)(2,1)}, u32[]{:S(2)}, u32[]{:S(2)}) collective-permute-start(bf16[800,128]{1,0:T(8,128)(2,1)S(1)} %get-tuple-element.34), channel_id=1, source_target_pairs={{0,8},{1,9},{16,24},{17,25},{32,40},{33,41},{48,56},{49,57},{64,72... | collective-permute-start | bytes 614408 | tf_op jit(solution)/shard_map/ppermute | solution.py:37
  37.9 16.1 %copy-start.7 = (pred[2]{0:T(512)(128)(4,1)}, pred[2]{0:T(512)(128)(4,1)S(1)}, u32[]{:S(2)}) copy-start(pred[2]{0:T(512)(128)(4,1)S(1)} %get-tuple-element.46) | copy-start | bytes 10
  46.2 5.2 %collective-permute-start.4 = (bf16[488,128]{1,0:T(8,128)(2,1)S(1)}, bf16[488,128]{1,0:T(8,128)(2,1)S(1)}, u32[]{:S(2)}, u32[]{:S(2)}) collective-permute-start(bf16[488,128]{1,0:T(8,128)(2,1)S(1)} %get-tuple-element.31), channel_id=1, source_target_pairs={{0,2},{4,6},{8,10},{12,14},{1,15},{5,3},{9,7},{13,11},{16,18},{20,... | collective-permute-start | bytes 374792 | tf_op jit(solution)/shard_map/ppermute | solution.py:57
  47.5 5.6 %collective-permute-start.3 = (bf16[488,128]{1,0:T(8,128)(2,1)S(1)}, bf16[488,128]{1,0:T(8,128)(2,1)S(1)}, u32[]{:S(2)}, u32[]{:S(2)}) collective-permute-start(bf16[488,128]{1,0:T(8,128)(2,1)S(1)} %get-tuple-element.32), channel_id=1, source_target_pairs={{0,1},{4,5},{8,9},{12,13},{1,0},{5,4},{9,8},{13,12},{16,17},{20,21... | collective-permute-start | bytes 374792 | tf_op jit(solution)/shard_map/ppermute | solution.py:54
  49.5 3.7 %collective-permute-start.5 = (bf16[488,128]{1,0:T(8,128)(2,1)S(1)}, bf16[488,128]{1,0:T(8,128)(2,1)S(1)}, u32[]{:S(2)}, u32[]{:S(2)}) collective-permute-start(bf16[488,128]{1,0:T(8,128)(2,1)S(1)} %get-tuple-element.33), channel_id=1, source_target_pairs={{0,15},{4,3},{8,7},{12,11},{1,2},{5,6},{9,10},{13,14},{16,31},{20,... | collective-permute-start | bytes 374792 | tf_op jit(solution)/shard_map/ppermute | solution.py:62
  87.4 27.6 %all-to-all-start.1 = ((bf16[32,64,128]{2,1,0:T(8,128)(2,1)}), bf16[32,64,128]{2,1,0:T(8,128)(2,1)}, u32[]{:S(2)}, u32[]{:S(2)}) async-start(bf16[32,64,128]{2,1,0:T(8,128)(2,1)} %broadcast_in_dim.150), calls=%async_computation.1 | async-start | bytes 1048576 | tf_op jit(solution)/shard_map/all_to_all | solution.py:108
  102.5 1.2 copy-start
  124.0 6.4 %copy-start.8 = (pred[2]{0:T(512)(128)(4,1)S(1)}, pred[2]{0:T(512)(128)(4,1)}, u32[]{:S(2)}) copy-start(pred[2]{0:T(512)(128)(4,1)} %copy-done.7) | copy-start | bytes 10
  126.2 4.2 %copy-start.5 = (bf16[128,512,1]{1,0,2:T(8,128)(2,1)S(1)}, bf16[128,512,1]{1,0,2:T(8,128)(2,1)}, u32[]{:S(2)}) copy-start(bf16[128,512,1]{1,0,2:T(8,128)(2,1)} %fusion.27) | copy-start | bytes 393220
  126.2 4.2 %copy-start.6 = (bf16[1,32,16,128]{3,2,0,1:T(8,128)(2,1)S(1)}, bf16[1,32,16,128]{3,2,0,1:T(8,128)(2,1)}, u32[]{:S(2)}) copy-start(bf16[1,32,16,128]{3,2,0,1:T(8,128)(2,1)} %get-tuple-element.14) | copy-start | bytes 393220
  126.2 6.0 %copy-start.1 = (bf16[2,512,128]{1,2,0:T(8,128)(2,1)S(1)}, bf16[2,512,128]{1,2,0:T(8,128)(2,1)}, u32[]{:S(2)}) copy-start(bf16[2,512,128]{1,2,0:T(8,128)(2,1)} %fusion.21) | copy-start | bytes 786436
  132.2 3.1 %copy-start.3 = (bf16[2,2,512,128]{3,2,1,0:T(8,128)(2,1)S(1)}, bf16[2,2,512,128]{3,2,1,0:T(8,128)(2,1)}, u32[]{:S(2)}) copy-start(bf16[2,2,512,128]{3,2,1,0:T(8,128)(2,1)} %copy.125) | copy-start | bytes 1572868
  132.2 3.1 %copy-start.4 = (bf16[2,2,512,128]{3,2,1,0:T(8,128)(2,1)S(1)}, bf16[2,2,512,128]{3,2,1,0:T(8,128)(2,1)}, u32[]{:S(2)}) copy-start(bf16[2,2,512,128]{3,2,1,0:T(8,128)(2,1)} %copy.126) | copy-start | bytes 1572868
Sparse Core Ops, SparseCore 0:
  54.1 63.0 all-gather.2

commit v2 on v0

v2 whole, which is shorter than its diff:
```python
import jax
import jax.numpy as jnp
from jax import lax
from jax.experimental import pallas as pl
from jax.experimental.pallas import tpu as pltpu
from jax.sharding import PartitionSpec as P

N_COL = 16
N_ROW = 32
PIECE = 256
MAIN = 240
REST = PIECE - MAIN
VMEM = pl.BlockSpec(memory_space=pltpu.VMEM)
SMEM = pl.BlockSpec(memory_space=pltpu.SMEM)
BF16 = jnp.bfloat16


def params():
    return pltpu.CompilerParams(vmem_limit_bytes=40 * 1024 * 1024)


def tn(first, second):
    return lax.dot_general(
        first, second, (((0,), (0,)), ((), ())), preferred_element_type=jnp.float32
    )


def nn(first, second):
    return jnp.dot(first, second, preferred_element_type=jnp.float32)


def nt(first, second):
    return lax.dot_general(
        first, second, (((1,), (1,)), ((), ())), preferred_element_type=jnp.float32
    )


def keep_if(condition, value):
    return jnp.where(condition, value, jnp.zeros_like(value))


def prepare_body(place, ranks, left, right, left_out, right_out, own, near, back, far, top):
    column = lax.broadcasted_iota(jnp.int32, (512, 128), 1)
    for a in range(2):
        for b in range(2):
            keep = column < ranks[2 * a + b]
            left_out[a, b] = jnp.where(keep, left[a, b], jnp.zeros_like(left[a, b]))
            right_out[a, b] = jnp.where(keep, right[a, b], jnp.zeros_like(right[a, b]))
    at_zero = place[1] == 0
    left_one, right_one = left_out[1, 0], right_out[1, 0]
    own[:512] = left_out[0, 0]
    near[:512] = jnp.where(at_zero, left_one, right_one)
    back[:512] = jnp.where(at_zero, right_one, left_one)
    far[:512] = right_out[0, 0]
    for k in range(8):
        tile = (left_out if k < 4 else right_out)[k // 2 % 2, 0]
        rest = tile[PIECE * (k % 2) + MAIN : PIECE * (k % 2 + 1)]
        for message in (own, near, back, far):
            message[512 + REST * k : 512 + REST * (k + 1)] = rest
    for b in range(2):
        top[:, b] = left_out[0, b].reshape(N_ROW, 16, 128)
        top[:, 2 + b] = right_out[0, b].reshape(N_ROW, 16, 128)


def prepare(place, ranks, left, right):
    message = jax.ShapeDtypeStruct((512 + 8 * REST, 128), BF16)
    four = jax.ShapeDtypeStruct((2, 2, 512, 128), BF16)
    return pl.pallas_call(
        prepare_body,
        out_shape=(four, four, message, message, message, message,
                   jax.ShapeDtypeStruct((N_ROW, 4, 16, 128), BF16)),
        in_specs=[SMEM, SMEM, VMEM, VMEM],
        out_specs=[VMEM] * 7,
        compiler_params=params(),
        cost_estimate=pl.CostEstimate(flops=10**6, bytes_accessed=3 * 2**20, transcendentals=0),
        name="prepare",
    )(place, ranks, left, right)


def update_body(
    place, left, right, main, mine, other, rows, inverses, out,
    got_left, got_lower, tall, second, update, wide, upper,
):
    p, q = place[0], place[1]
    step = pl.program_id(0)
    a, b = step // 2, step % 2

    def row_tile(t):
        return rows[:, t].reshape(512, 128)

    @pl.when(step == 0)
    def _():
        even = q % 2 == 0
        rests = (
            jnp.where(even, mine[...], other[...]),
            jnp.where(even, other[...], mine[...]),
        )

        def column_tile(panel, tile):
            parts = []
            for k in (2 * tile, 2 * tile + 1):
                parts += [main[2 * k + panel], rests[panel][REST * k : REST * (k + 1)]]
            return jnp.concatenate(parts, axis=0)

        left_ten, right_ten, left_one, right_one = [row_tile(8 + k) for k in range(4)]
        pivot = tn(inverses[1], right_one).astype(BF16)
        lower_ten = tn(inverses[0], right_ten).astype(BF16)
        for k in range(2):
            got_left[k] = column_tile(0, k)
            got_lower[k] = tn(inverses[0], column_tile(0, 2 + k)).astype(BF16)
            tall[k, :, :128] = column_tile(1, k)
            second[k, :, :128] = tn(inverses[1], column_tile(1, 2 + k)).astype(BF16)
            second[k, :, 128:] = pivot
            middle = keep_if((k > 0) | (p > 0), tn(got_lower[k], left_one)).astype(BF16)
            tall[k, :, 128:] = -nn(got_left[k], middle).astype(BF16)
            middle = keep_if((k > 0) | (q > 0), tn(lower_ten, row_tile(k))).astype(BF16)
            wide[k, :, :128] = row_tile(4 + k)
            wide[k, :, 128:] = -nn(left_ten, middle).astype(BF16)
            upper[k, :, :128] = row_tile(6 + k)
            upper[k, :, 128:] = row_tile(2 + k)
        for i in range(2):
            for j in range(2):
                keep = ((i > 0) | (p > 0)) & ((j > 0) | (q > 0))
                middle = keep_if(keep, tn(got_lower[i], row_tile(j))).astype(BF16)
                update[i, j] = -nn(got_left[i], middle).astype(BF16)

    row = a * N_ROW + p
    col = b * N_COL + q
    middle = keep_if((row > 1) & (col > 1), tn(second[a], wide[b])).astype(BF16)
    change = -nn(tall[a], middle).astype(BF16)
    is_first = (col == 0) & (row > 0)
    is_second = (col == 1) & (row > 1)
    near = jnp.where(
        is_first, got_lower[a], jnp.where(is_second, second[a, :, :128], right[a, b])
    )
    beside = jnp.where(is_second, second[a, :, 128:], upper[b, :, 128:])
    all_left = jnp.concatenate([left[a, b], update[a, b], change], axis=1)
    all_right = jnp.concatenate([near, beside, upper[b]], axis=1)
    out[0] = nt(all_left, all_right).astype(BF16)


def update_tiles(place, left, right, main, mine, other, rows, inverses):
    pair, double = (2, 512, 128), (2, 512, 256)
    return pl.pallas_call(
        update_body,
        grid=(4,),
        out_shape=jax.ShapeDtypeStruct((4, 512, 512), BF16),
        in_specs=[SMEM] + [VMEM] * 7,
        out_specs=pl.BlockSpec((1, 512, 512), lambda s: (s, 0, 0)),
        scratch_shapes=[
            pltpu.VMEM(shape, BF16)
            for shape in (pair, pair, double, double, (2, 2, 512, 128), double, double)
        ],
        compiler_params=params(),
        cost_estimate=pl.CostEstimate(
            flops=25 * 10**8, bytes_accessed=8 * 2**20, transcendentals=0
        ),
        name="update_tiles",
    )(place, left, right, main, mine, other, rows, inverses)


def to_all(block, axis, size):
    sent = jnp.broadcast_to(block[None], (size,) + block.shape)
    return lax.all_to_all(sent, axis, 0, 0, tiled=True)


def per_device(left_factors, right_factors, ranks, pivot_inverses):
    shape_four = (2, 2, 512, 128)
    p = lax.axis_index("row")
    q = lax.axis_index("col")
    place = jnp.stack([p, q]).astype(jnp.int32)
    left, right, own, near, back, far, top = prepare(
        place, ranks.reshape(4), left_factors.reshape(shape_four), right_factors.reshape(shape_four)
    )
    scattered = lax.all_to_all(top, "row", 0, 0, tiled=True)[:2]
    near = lax.ppermute(near, "col", [(0, 4), (1, 13)])
    back = lax.ppermute(back, "col", [(0, 12), (1, 5)])
    far = lax.ppermute(far, "col", [(0, 8), (1, 9)])

    corner = jnp.where(q == 0, scattered[1], scattered[0])
    corner = to_all(jnp.concatenate([corner[0], corner[2]], axis=0), "col", N_COL)
    corner = corner.reshape(N_COL, 32, 128)[:2].reshape(64, 128)

    head = jnp.where(
        q < 2,
        own,
        jnp.where((q == 4) | (q == 13), near, jnp.where((q == 12) | (q == 5), back, far)),
    )
    moved = lax.ppermute(
        head[PIECE:], "col", [(s + c, s + c + 2) for s in range(0, N_COL, 4) for c in range(2)]
    )
    kept = q % 4 < 2
    piece = jnp.where(kept, head[:MAIN], moved[:MAIN])
    mine = jnp.where(kept, head[512:], moved[PIECE:])
    other = lax.ppermute(mine, "col", [(i, i ^ 1) for i in range(N_COL)])

    block = jnp.concatenate([scattered.reshape(128, 128), corner], axis=0)
    block, piece = lax.optimization_barrier((block, piece))
    rows = to_all(block, "row", N_ROW).reshape(N_ROW, 12, 16, 128)
    main = lax.all_gather(piece, "col")
    dense = update_tiles(place, left, right, main, mine, other, rows, pivot_inverses)
    return dense.reshape(2, 1, 2, 1, 512, 512)


def solution(mesh):
    in_specs = (
        P(None, "row", None, "col", None, None),
        P(None, "row", None, "col", None, None),
        P(None, "row", None, "col"),
        P(),
    )
    out_specs = P(None, "row", None, "col", None, None)
    return jax.shard_map(
        per_device, mesh=mesh, in_specs=in_specs, out_specs=out_specs, check_vma=False
    )
```

time: 583 us -> 109 us (0.19)
  the two profiles are of different devices: /device:TPU:2 before, /device:TPU:4 now
where the time goes in v2:
time: 109 us; the launch traced here: 108 us
  starting transfers between devices  45.2 us (41%)
  blocking collectives  33.9 us (31%)
  waiting for transfers between devices  10.8 us (10%)
  Pallas kernels  8.61 us (8%)
  local copies, waits for them, and re-layouts  7.98 us (7%)
  other arithmetic  1.46 us (1%)
    all_gather x1, blocking collectives, per_device(): main = lax.all_gather(piece, 'col')  33.9 us
    all_to_all x2, starting transfers between devices, to_all(): return lax.all_to_all(sent, axis, 0, 0, tiled=True)  13.8 us
    all_to_all x1, starting transfers between devices, per_device(): scattered = lax.all_to_all(top, 'row', 0, 0, tiled=True)[:2]  9.44 us
    ppermute x1, starting transfers between devices, per_device(): near = lax.ppermute(near, 'col', [(0, 4), (1, 13)])  7.25 us
    pallas_call x1, Pallas kernels, update_tiles(): pl.pallas_call(update_body, grid=(4,), out_shape=jax.ShapeDtypeStruct((4,...  6.88 us
    all_to_all x2, waiting for transfers between devices, to_all(): return lax.all_to_all(sent, axis, 0, 0, tiled=True)  6.76 us
    unnamed x11, local copies, waits for them, and re-layouts  5.71 us
    ppermute x1, starting transfers between devices, per_device(): lax.ppermute(head[PIECE:], 'col', [(s + c, s + c + 2) for s in range(0, N...  4.73 us
  transfers between devices with their start and end apart: 8, of which 2 were waited for; matrix products, arithmetic and copies ran while one was open for 1% of the time, Pallas kernels for 0%

profile of v2, /device:TPU:4, one launch (start us, length us, event | category | flops | bytes accessed | tf_op | source)
XLA Modules:
  0.0 108.1 jit_solution(17099923913082543881)
XLA Ops:
  0.0 0.6 broadcast.8
  0.6 1.3 %reduce.3 = s32[2,2]{1,0:T(2,128)S(1)} reduce(s32[2,1,2,1]{2,3,1,0:T(1,128)} %param.6, s32[]{:T(128)} %broadcast.8), dimensions={1,3}, to_apply=%param.6.reduce_sub_computation.3 | reduce | bytes 36 | tf_op args[2]
  1.9 0.1 reshape.29.ranks
  2.0 0.1 pad_add_fusion.place
  2.1 1.0 copy-done
  3.1 1.0 copy-done.1
  4.1 1.7 %prepare.1 = (bf16[2,2,512,128]{3,2,1,0:T(8,128)(2,1)S(1)}, bf16[2,2,512,128]{3,2,1,0:T(8,128)(2,1)S(1)}, bf16[640,128]{1,0:T(8,128)(2,1)S(1)}, bf16[640,128]{1,...) custom-call(s32[2]{0:T(128)S(1)} %pad_add_fusion.place, ...), custom_call_target="tpu_custom_call" | custom-call | flops 1000000 | bytes 3145728 | tf_op jit(solution)/shard_map/prepare/pallas_call | solution.py:68
  5.9 0.8 copy-done.3
  6.7 9.4 %all-to-all-start = ((bf16[32,4,16,128]{3,2,1,0:T(8,128)(2,1)}), bf16[32,4,16,128]{3,2,1,0:T(8,128)(2,1)S(1)}, u32[]{:S(2)}, u32[]{:S(2)}) async-start(bf16[32,4,16,128]{3,2,1,0:T(8,128)(2,1)} %get-tuple-element.16), calls=%async_computation | async-start | bytes 1048576 | tf_op jit(solution)/shard_map/all_to_all | solution.py:175
  16.1 7.3 %collective-permute-start = (bf16[640,128]{1,0:T(8,128)(2,1)S(1)}, bf16[640,128]{1,0:T(8,128)(2,1)S(1)}, u32[]{:S(2)}, u32[]{:S(2)}) collective-permute-start(bf16[640,128]{1,0:T(8,128)(2,1)S(1)} %get-tuple-element.18), channel_id=1, source_target_pairs={{0,4},{1,13},{16,20},{17,29},{32,36},{33,45},{48,52},{49,61},{64,6... | collective-permute-start | bytes 491528 | tf_op jit(solution)/shard_map/ppermute | solution.py:176
  23.4 4.3 %collective-permute-start.1 = (bf16[640,128]{1,0:T(8,128)(2,1)S(1)}, bf16[640,128]{1,0:T(8,128)(2,1)S(1)}, u32[]{:S(2)}, u32[]{:S(2)}) collective-permute-start(bf16[640,128]{1,0:T(8,128)(2,1)S(1)} %get-tuple-element.19), channel_id=1, source_target_pairs={{0,12},{1,5},{16,28},{17,21},{32,44},{33,37},{48,60},{49,53},{64,7... | collective-permute-start | bytes 491528 | tf_op jit(solution)/shard_map/ppermute | solution.py:177
  27.7 3.7 %collective-permute-start.2 = (bf16[640,128]{1,0:T(8,128)(2,1)S(1)}, bf16[640,128]{1,0:T(8,128)(2,1)S(1)}, u32[]{:S(2)}, u32[]{:S(2)}) collective-permute-start(bf16[640,128]{1,0:T(8,128)(2,1)S(1)} %get-tuple-element.20), channel_id=1, source_target_pairs={{0,8},{1,9},{16,24},{17,25},{32,40},{33,41},{48,56},{49,57},{64,72... | collective-permute-start | bytes 491528 | tf_op jit(solution)/shard_map/ppermute | solution.py:178
  31.4 0.7 broadcast_in_dim.4
  32.1 7.7 %all-to-all-start.1 = ((bf16[16,32,128]{2,1,0:T(8,128)(2,1)}), bf16[16,32,128]{2,1,0:T(8,128)(2,1)S(1)}, u32[]{:S(2)}, u32[]{:S(2)}) async-start(bf16[16,32,128]{2,1,0:T(8,128)(2,1)} %broadcast_in_dim.4), calls=%async_computation.1 | async-start | bytes 262144 | tf_op jit(solution)/shard_map/all_to_all | solution.py:164
  39.9 4.7 %collective-permute-start.3 = (bf16[384,128]{1,0:T(8,128)(2,1)S(1)}, bf16[384,128]{1,0:T(8,128)(2,1)S(1)}, u32[]{:S(2)}, u32[]{:S(2)}) collective-permute-start(bf16[384,128]{1,0:T(8,128)(2,1)S(1)} %slice.55), channel_id=1, source_target_pairs={{0,2},{1,3},{4,6},{5,7},{8,10},{9,11},{12,14},{13,15},{16,18},{17,... | collective-permute-start | bytes 294920 | tf_op jit(solution)/shard_map/ppermute | solution.py:189
  44.7 4.0 %collective-permute-done.3 = bf16[384,128]{1,0:T(8,128)(2,1)S(1)} collective-permute-done((bf16[384,128]{1,0:T(8,128)(2,1)S(1)}, bf16[384,128]{1,0:T(8,128)(2,1)S(1)}, u32[]{:S(2)}, u32[]{:S(2)}) %collective-permute-start.3) | collective-permute-done | bytes 98336 | tf_op jit(solution)/shard_map/ppermute | solution.py:189
  48.7 6.8 %all-to-all-done.1 = bf16[16,32,128]{2,1,0:T(8,128)(2,1)S(1)} async-done(((bf16[16,32,128]{2,1,0:T(8,128)(2,1)}), bf16[16,32,128]{2,1,0:T(8,128)(2,1)S(1)}, u32[]{:S(2)}, u32[]{:S(2)}) %all-to-all-start.1) | async-done | bytes 131104 | tf_op jit(solution)/shard_map/all_to_all | solution.py:164
  55.5 1.5 %broadcast_in_dim.5 = bf16[32,192,128]{2,1,0:T(8,128)(2,1)} broadcast(bf16[192,128]{1,0:T(8,128)(2,1)S(1)} %pad_maximum_fusion), dimensions={1,2} | broadcast | bytes 1622016 | tf_op jit(solution)/shard_map/broadcast_in_dim | solution.py:163
  57.0 6.0 %all-to-all-start.2 = ((bf16[32,192,128]{2,1,0:T(8,128)(2,1)}), bf16[32,192,128]{2,1,0:T(8,128)(2,1)S(1)}, u32[]{:S(2)}, u32[]{:S(2)}) async-start(bf16[32,192,128]{2,1,0:T(8,128)(2,1)} %broadcast_in_dim.5), calls=%async_computation.2 | async-start | bytes 3145728 | tf_op jit(solution)/shard_map/all_to_all | solution.py:164
  63.0 2.1 %collective-permute-start.4 = (bf16[128,128]{1,0:T(8,128)(2,1)S(1)}, bf16[128,128]{1,0:T(8,128)(2,1)S(1)}, u32[]{:S(2)}, u32[]{:S(2)}) collective-permute-start(bf16[128,128]{1,0:T(8,128)(2,1)S(1)} %slice_select_fusion.1.mine), channel_id=1, source_target_pairs={{0,1},{1,0},{2,3},{3,2},{4,5},{5,4},{6,7},{7,6},{8,9},{9,8},{10,11... | collective-permute-start | bytes 98312 | tf_op jit(solution)/shard_map/ppermute | solution.py:195
  65.1 33.9 %all-gather = bf16[3840,128]{1,0:T(8,128)(2,1)S(1)} all-gather(bf16[240,128]{1,0:T(8,128)(2,1)S(1)} %slice_select_fusion), channel_id=2, replica_groups=mesh['row'=32,'col'=16] {'col'}, dimensions={0}, use_global_device_ids=true | all-gather | bytes 1044480 | tf_op jit(solution)/shard_map/all_gather | solution.py:200
  99.0 1.2 %copy-done.2 = bf16[2,512,512]{2,1,0:T(8,128)(2,1)S(1)} copy-done((bf16[2,512,512]{2,1,0:T(8,128)(2,1)S(1)}, bf16[2,512,512]{2,1,0:T(8,128)(2,1)}, u32[]{:S(2)}) %copy-start.2) | copy-done | bytes 1048600
  100.2 1.0 copy-done.4
  101.3 6.9 %update_tiles.1 = bf16[4,512,512]{2,1,0:T(8,128)(2,1)} custom-call(s32[2]{0:T(128)S(1)} %pad_add_fusion.place, bf16[2,2,512,128]{3,2,1,0:T(8,128)(2,1)S(1)} %get-tuple-element.14.left, bf16[2,2,512,128]{3,2,1,0:T(8,128)(2,1)S(1)} %copy-done.4, bf16[16,240,128]{2,1,0:T(8,128)(2,1)S(1)} %bitcast.17, bf16[128,128]{1,0:T(8,128)(2,1)S(1)} %slice_select_fusion.1.mine, ...), custom_call_target="tpu_custom_call" | custom-call | flops 2500000000 | bytes 8388608 | tf_op jit(solution)/shard_map/update_tiles/pallas_call | solution.py:144
  (21 shorter events, 0.1 us)
Async XLA Ops:
  2.0 1.0 copy-start
  3.1 1.0 copy-start.1
  5.9 0.8 copy-start.3
  6.7 24.7 %all-to-all-start = ((bf16[32,4,16,128]{3,2,1,0:T(8,128)(2,1)}), bf16[32,4,16,128]{3,2,1,0:T(8,128)(2,1)S(1)}, u32[]{:S(2)}, u32[]{:S(2)}) async-start(bf16[32,4,16,128]{3,2,1,0:T(8,128)(2,1)} %get-tuple-element.16), calls=%async_computation | async-start | bytes 1048576 | tf_op jit(solution)/shard_map/all_to_all | solution.py:175
  16.1 23.7 %collective-permute-start = (bf16[640,128]{1,0:T(8,128)(2,1)S(1)}, bf16[640,128]{1,0:T(8,128)(2,1)S(1)}, u32[]{:S(2)}, u32[]{:S(2)}) collective-permute-start(bf16[640,128]{1,0:T(8,128)(2,1)S(1)} %get-tuple-element.18), channel_id=1, source_target_pairs={{0,4},{1,13},{16,20},{17,29},{32,36},{33,45},{48,52},{49,61},{64,6... | collective-permute-start | bytes 491528 | tf_op jit(solution)/shard_map/ppermute | solution.py:176
  23.4 16.5 %collective-permute-start.1 = (bf16[640,128]{1,0:T(8,128)(2,1)S(1)}, bf16[640,128]{1,0:T(8,128)(2,1)S(1)}, u32[]{:S(2)}, u32[]{:S(2)}) collective-permute-start(bf16[640,128]{1,0:T(8,128)(2,1)S(1)} %get-tuple-element.19), channel_id=1, source_target_pairs={{0,12},{1,5},{16,28},{17,21},{32,44},{33,37},{48,60},{49,53},{64,7... | collective-permute-start | bytes 491528 | tf_op jit(solution)/shard_map/ppermute | solution.py:177
  27.7 12.2 %collective-permute-start.2 = (bf16[640,128]{1,0:T(8,128)(2,1)S(1)}, bf16[640,128]{1,0:T(8,128)(2,1)S(1)}, u32[]{:S(2)}, u32[]{:S(2)}) collective-permute-start(bf16[640,128]{1,0:T(8,128)(2,1)S(1)} %get-tuple-element.20), channel_id=1, source_target_pairs={{0,8},{1,9},{16,24},{17,25},{32,40},{33,41},{48,56},{49,57},{64,72... | collective-permute-start | bytes 491528 | tf_op jit(solution)/shard_map/ppermute | solution.py:178
  32.1 23.4 %all-to-all-start.1 = ((bf16[16,32,128]{2,1,0:T(8,128)(2,1)}), bf16[16,32,128]{2,1,0:T(8,128)(2,1)S(1)}, u32[]{:S(2)}, u32[]{:S(2)}) async-start(bf16[16,32,128]{2,1,0:T(8,128)(2,1)} %broadcast_in_dim.4), calls=%async_computation.1 | async-start | bytes 262144 | tf_op jit(solution)/shard_map/all_to_all | solution.py:164
  39.9 8.7 %collective-permute-start.3 = (bf16[384,128]{1,0:T(8,128)(2,1)S(1)}, bf16[384,128]{1,0:T(8,128)(2,1)S(1)}, u32[]{:S(2)}, u32[]{:S(2)}) collective-permute-start(bf16[384,128]{1,0:T(8,128)(2,1)S(1)} %slice.55), channel_id=1, source_target_pairs={{0,2},{1,3},{4,6},{5,7},{8,10},{9,11},{12,14},{13,15},{16,18},{17,... | collective-permute-start | bytes 294920 | tf_op jit(solution)/shard_map/ppermute | solution.py:189
  57.0 42.0 %all-to-all-start.2 = ((bf16[32,192,128]{2,1,0:T(8,128)(2,1)}), bf16[32,192,128]{2,1,0:T(8,128)(2,1)S(1)}, u32[]{:S(2)}, u32[]{:S(2)}) async-start(bf16[32,192,128]{2,1,0:T(8,128)(2,1)} %broadcast_in_dim.5), calls=%async_computation.2 | async-start | bytes 3145728 | tf_op jit(solution)/shard_map/all_to_all | solution.py:164
  63.0 36.0 %collective-permute-start.4 = (bf16[128,128]{1,0:T(8,128)(2,1)S(1)}, bf16[128,128]{1,0:T(8,128)(2,1)S(1)}, u32[]{:S(2)}, u32[]{:S(2)}) collective-permute-start(bf16[128,128]{1,0:T(8,128)(2,1)S(1)} %slice_select_fusion.1.mine), channel_id=1, source_target_pairs={{0,1},{1,0},{2,3},{3,2},{4,5},{5,4},{6,7},{7,6},{8,9},{9,8},{10,11... | collective-permute-start | bytes 98312 | tf_op jit(solution)/shard_map/ppermute | solution.py:195
  99.0 1.2 %copy-start.2 = (bf16[2,512,512]{2,1,0:T(8,128)(2,1)S(1)}, bf16[2,512,512]{2,1,0:T(8,128)(2,1)}, u32[]{:S(2)}) copy-start(bf16[2,512,512]{2,1,0:T(8,128)(2,1)} %inverses.1) | copy-start | bytes 3145732
  100.2 1.0 copy-start.4

commit v3 on v2

v3 whole, which is shorter than its diff:
```python
import jax
import jax.numpy as jnp
from jax import lax
from jax.experimental import pallas as pl
from jax.experimental.pallas import tpu as pltpu
from jax.sharding import PartitionSpec as P

N_COL = 16
N_ROW = 32
PIECE = 256
MAIN = 240
REST = PIECE - MAIN
HOLDERS = ((0, 14, 2, 4, 6, 8, 12, 10), (1, 3, 5, 7, 11, 9, 15, 13))
VMEM = pl.BlockSpec(memory_space=pltpu.VMEM)
SMEM = pl.BlockSpec(memory_space=pltpu.SMEM)
HBM = pl.BlockSpec(memory_space=pltpu.HBM)
BF16 = jnp.bfloat16


def params():
    return pltpu.CompilerParams(vmem_limit_bytes=24 * 1024 * 1024)


def cost(flops, size):
    return pl.CostEstimate(flops=flops, bytes_accessed=size, transcendentals=0)


def tn(first, second):
    return lax.dot_general(
        first, second, (((0,), (0,)), ((), ())), preferred_element_type=jnp.float32
    )


def nn(first, second):
    return jnp.dot(first, second, preferred_element_type=jnp.float32)


def nt(first, second):
    return lax.dot_general(
        first, second, (((1,), (1,)), ((), ())), preferred_element_type=jnp.float32
    )


def mask_rank(tile, rank):
    column = lax.broadcasted_iota(jnp.int32, (512, 128), 1)
    return jnp.where(column < rank, tile, jnp.zeros_like(tile))


def in_hbm(*arrays):
    return [pltpu.with_memory_space_constraint(x, pltpu.HBM) for x in arrays]


def fetch(pairs, arrived):
    copies = [
        pltpu.make_async_copy(source, target, arrived.at[k])
        for k, (source, target) in enumerate(pairs)
    ]
    for copy in copies:
        copy.start()
    return copies


def top_body(ranks, left, right, top, left_row, right_row, arrived):
    pairs = ((left.at[0, 0, :, 0], left_row), (right.at[0, 0, :, 0], right_row))
    for k, copy in enumerate(fetch(pairs, arrived)):
        copy.wait()
        for b in range(2):
            tile = mask_rank(pairs[k][1][b], ranks[0, 0, 0, b])
            top[:, 2 * k + b] = tile.reshape(N_ROW, 16, 128)


def top_rows(ranks, left, right):
    return pl.pallas_call(
        top_body,
        out_shape=jax.ShapeDtypeStruct((N_ROW, 4, 16, 128), BF16),
        in_specs=[SMEM, HBM, HBM],
        out_specs=VMEM,
        scratch_shapes=[pltpu.VMEM((2, 512, 128), BF16)] * 2 + [pltpu.SemaphoreType.DMA((2,))],
        compiler_params=params(),
        cost_estimate=cost(10**6, 2**20),
        name="top_rows",
    )(ranks, *in_hbm(left, right))


def messages_body(
    place, ranks, left, right, own, near, middle, far, left_col, right_col, arrived
):
    pairs = ((left.at[:, 0, 0, 0], left_col), (right.at[:, 0, 0, 0], right_col))
    for copy in fetch(pairs, arrived):
        copy.wait()
    tiles = [mask_rank(ref[a], ranks[a, 0, 0, 0]) for ref in (left_col, right_col) for a in range(2)]
    at_zero = place[1] == 0
    own[:512] = tiles[0]
    near[:512] = jnp.where(at_zero, tiles[1], tiles[3])
    middle[:512] = jnp.where(at_zero, tiles[3], tiles[1])
    far[:512] = tiles[2]
    for k in range(8):
        rest = tiles[k // 2][PIECE * (k % 2) + MAIN : PIECE * (k % 2 + 1)]
        for message in (own, near, middle, far):
            message[512 + REST * k : 512 + REST * (k + 1)] = rest


def messages(place, ranks, left, right):
    message = jax.ShapeDtypeStruct((512 + 8 * REST, 128), BF16)
    return pl.pallas_call(
        messages_body,
        out_shape=(message,) * 4,
        in_specs=[SMEM, SMEM, HBM, HBM],
        out_specs=[VMEM] * 4,
        scratch_shapes=[pltpu.VMEM((2, 512, 128), BF16)] * 2 + [pltpu.SemaphoreType.DMA((2,))],
        compiler_params=params(),
        cost_estimate=cost(10**6, 2**20),
        name="messages",
    )(place, ranks, *in_hbm(left, right))


def update_body(
    place, ranks, left_hbm, right_hbm, main_hbm, inverses_hbm, mine, other, rows, out,
    left, right, main, inverses, arrived, lowers, ups, second, wide, tall, upper, update, change,
):
    p, q = place[0], place[1]
    step = pl.program_id(0)
    a, b = step // 2, step % 2

    def row_tile(t):
        return rows[:, t].reshape(512, 128)

    @pl.when(step == 0)
    def _():
        pairs = (
            (main_hbm, main),
            (inverses_hbm, inverses),
            (left_hbm.at[:, 0, :, 0], left),
            (right_hbm.at[:, 0, :, 0], right),
        )
        copies = fetch(pairs, arrived)
        copies[0].wait()
        copies[1].wait()
        even = q % 2 == 0
        rests = (
            jnp.where(even, mine[...], other[...]),
            jnp.where(even, other[...], mine[...]),
        )

        def column_tile(panel, tile):
            parts = []
            for k in (2 * tile, 2 * tile + 1):
                parts += [main[HOLDERS[panel][k]], rests[panel][REST * k : REST * (k + 1)]]
            return jnp.concatenate(parts, axis=0)

        raw = jnp.concatenate([column_tile(0, 2), column_tile(0, 3), row_tile(9)], axis=1)
        lowers[...] = tn(inverses[0], raw).astype(BF16)
        ups[...] = jnp.concatenate([row_tile(0), row_tile(1), row_tile(10)], axis=1)
        raw = jnp.concatenate([column_tile(1, 2), column_tile(1, 3), row_tile(11)], axis=1)
        fresh = tn(inverses[1], raw).astype(BF16)
        second[:, :128] = fresh[:, :128]
        second[:, 128:256] = fresh[:, 256:]
        second[:, 256:384] = fresh[:, 128:256]
        second[:, 384:] = fresh[:, 256:]

        line = lax.broadcasted_iota(jnp.int32, (384, 384), 0)
        column = lax.broadcasted_iota(jnp.int32, (384, 384), 1)
        drop = ((line < 128) & (p == 0)) | ((column < 128) & (q == 0))
        product = tn(lowers[...], ups[...])
        inner = jnp.where(drop, 0.0, product).astype(BF16)
        for k in range(2):
            result = -nn(column_tile(0, k), inner[128 * k : 128 * (k + 1)])
            update[k] = result.astype(BF16)
            tall[k, :, :128] = column_tile(1, k)
            tall[k, :, 128:] = update[k, :, 256:]
            upper[k, :, :128] = row_tile(6 + k)
            upper[k, :, 128:] = row_tile(2 + k)
        result = -nn(row_tile(8), inner[256:, :256])
        for k in range(2):
            wide[:, 256 * k : 256 * k + 128] = row_tile(4 + k)
            wide[:, 256 * k + 128 : 256 * k + 256] = result[:, 128 * k : 128 * (k + 1)].astype(BF16)

        line = lax.broadcasted_iota(jnp.int32, (512, 512), 0)
        column = lax.broadcasted_iota(jnp.int32, (512, 512), 1)
        drop = ((line < 256) & (p <= 1)) | ((column < 256) & (q <= 1))
        product = tn(second[...], wide[...])
        inner = jnp.where(drop, 0.0, product).astype(BF16)
        for k in range(2):
            result = -nn(tall[k], inner[256 * k : 256 * (k + 1)])
            for j in range(2):
                change[k, j] = result[:, 256 * j : 256 * (j + 1)].astype(BF16)
        copies[2].wait()
        copies[3].wait()

    row = a * N_ROW + p
    col = b * N_COL + q
    rank = ranks[a, 0, 0, b]
    is_first = (col == 0) & (row > 0)
    is_second = (col == 1) & (row > 1)

    def pick(ref, width):
        return jnp.where(a == 0, ref[:, :128], ref[:, width : width + 128])

    near = jnp.where(
        is_first,
        pick(lowers, 128),
        jnp.where(is_second, pick(second, 256), mask_rank(right[a, b], rank)),
    )
    beside = jnp.where(is_second, second[:, 128:256], upper[b, :, 128:])
    done = jnp.where(b == 0, update[a, :, :128], update[a, :, 128:256])
    all_left = jnp.concatenate([mask_rank(left[a, b], rank), done, change[a, b]], axis=1)
    all_right = jnp.concatenate([near, beside, upper[b]], axis=1)
    out[0, 0, 0, 0] = nt(all_left, all_right).astype(BF16)


def update_tiles(place, ranks, left, right, main, mine, other, rows, inverses):
    four = pltpu.VMEM((2, 2, 512, 128), BF16)
    shapes = (
        (512, 384), (512, 384), (512, 512), (512, 512),
        (2, 512, 256), (2, 512, 256), (2, 512, 384), (2, 2, 512, 256),
    )
    return pl.pallas_call(
        update_body,
        grid=(4,),
        out_shape=jax.ShapeDtypeStruct((2, 1, 2, 1, 512, 512), BF16),
        in_specs=[SMEM, SMEM] + [HBM] * 4 + [VMEM] * 3,
        out_specs=pl.BlockSpec(
            (1, 1, 1, 1, 512, 512), lambda s: (s // 2, 0, s % 2, 0, 0, 0)
        ),
        scratch_shapes=[four, four, pltpu.VMEM((N_COL, MAIN, 128), BF16)]
        + [pltpu.VMEM((2, 512, 512), BF16), pltpu.SemaphoreType.DMA((4,))]
        + [pltpu.VMEM(shape, BF16) for shape in shapes],
        compiler_params=params(),
        cost_estimate=cost(25 * 10**8, 8 * 2**20),
        name="update_tiles",
    )(place, ranks, *in_hbm(left, right, main, inverses), mine, other, rows)


def to_all(block, axis, size):
    sent = jnp.broadcast_to(block[None], (size,) + block.shape)
    return lax.all_to_all(sent, axis, 0, 0, tiled=True)


def per_device(left, right, ranks, pivot_inverses):
    p = lax.axis_index("row")
    q = lax.axis_index("col")
    place = jnp.stack([p, q]).astype(jnp.int32)
    ranks = ranks.reshape(2, 1, 1, 2)
    top = top_rows(ranks, left, right)
    own, near, middle, far = messages(place, ranks, left, right)
    near = lax.ppermute(near, "col", [(0, 2), (1, 15)])
    middle = lax.ppermute(middle, "col", [(0, 12), (1, 5)])
    far = lax.ppermute(far, "col", [(0, 6), (1, 11)])
    scattered = lax.all_to_all(top, "row", 0, 0, tiled=True)[:2]

    corner = jnp.where(q == 0, scattered[1], scattered[0])
    corner = to_all(jnp.concatenate([corner[0], corner[2]], axis=0), "col", N_COL)
    corner = corner.reshape(N_COL, 32, 128)[:2].reshape(64, 128)

    by_near = (q == 2) | (q == 15)
    by_middle = (q == 12) | (q == 5)
    is_head = (q < 2) | by_near | by_middle | (q == 6) | (q == 11)
    head = jnp.where(q < 2, own, jnp.where(by_near, near, jnp.where(by_middle, middle, far)))
    hops = [(line[k], line[k + 1]) for line in HOLDERS for k in range(0, 8, 2)]
    moved = lax.ppermute(head[PIECE:], "col", hops)
    piece = jnp.where(is_head, head[:MAIN], moved[:MAIN])
    mine = jnp.where(is_head, head[512:], moved[PIECE:])
    other = lax.ppermute(mine, "col", [(i, i ^ 1) for i in range(N_COL)])

    block = jnp.concatenate([scattered.reshape(128, 128), corner], axis=0)
    block, piece = lax.optimization_barrier((block, piece))
    rows = to_all(block, "row", N_ROW).reshape(N_ROW, 12, 16, 128)
    main = lax.all_gather(piece, "col")
    return update_tiles(place, ranks, left, right, main, mine, other, rows, pivot_inverses)


def solution(mesh):
    in_specs = (
        P(None, "row", None, "col", None, None),
        P(None, "row", None, "col", None, None),
        P(None, "row", None, "col"),
        P(),
    )
    out_specs = P(None, "row", None, "col", None, None)
    return jax.shard_map(
        per_device, mesh=mesh, in_specs=in_specs, out_specs=out_specs, check_vma=False
    )
```

time: 109 us -> 106 us (0.972)
  the two profiles are of different devices: /device:TPU:4 before, /device:TPU:2 now
where the time goes in v3:
time: 106 us; the launch traced here: 105 us
  starting transfers between devices  46.2 us (44%)
  blocking collectives  35.4 us (33%)
  Pallas kernels  11.8 us (11%)
  waiting for transfers between devices  8.3 us (8%)
  local copies, waits for them, and re-layouts  2.94 us (3%)
    all_gather x1, blocking collectives, per_device(): main = lax.all_gather(piece, 'col')  35.4 us
    all_to_all x2, starting transfers between devices, to_all(): return lax.all_to_all(sent, axis, 0, 0, tiled=True)  14.5 us
    all_to_all x1, starting transfers between devices, per_device(): scattered = lax.all_to_all(top, 'row', 0, 0, tiled=True)[:2]  9.47 us
    ppermute x1, starting transfers between devices, per_device(): middle = lax.ppermute(middle, 'col', [(0, 12), (1, 5)])  8.23 us
    pallas_call x1, Pallas kernels, update_tiles(): pl.pallas_call(update_body, grid=(4,), out_shape=jax.ShapeDtypeStruct((2,...  7.58 us
    ppermute x1, starting transfers between devices, per_device(): moved = lax.ppermute(head[PIECE:], 'col', hops)  5.95 us
    all_to_all x2, waiting for transfers between devices, to_all(): return lax.all_to_all(sent, axis, 0, 0, tiled=True)  5.23 us
    ppermute x1, starting transfers between devices, per_device(): other = lax.ppermute(mine, 'col', [(i, i ^ 1) for i in range(N_COL)])  3.41 us
  transfers between devices with their start and end apart: 8, of which 2 were waited for; matrix products, arithmetic and copies ran while one was open for 1% of the time, Pallas kernels for 2%

profile of v3, /device:TPU:2, one launch (start us, length us, event | category | flops | bytes accessed | tf_op | source)
XLA Modules:
  0.0 105.0 jit_solution(13117644350381867273)
XLA Ops:
  0.0 0.7 copy-done
  0.8 2.4 %top_rows.1 = bf16[32,4,16,128]{3,2,1,0:T(8,128)(2,1)} custom-call(s32[2,1,1,2]{3,2,1,0:T(1,128)S(1)} %bitcast.14, bf16[2,1,2,1,512,128]{5,4,3,2,1,0:T(8,128)(2,1)} %left_hbm.1, bf16[2,1,2,1,512,128]{5,4,3,2,1,0:T(8,128)(2,1)} %right_hbm.1), custom_call_target="tpu_custom_call" | custom-call | flops 1000000 | bytes 1048576 | tf_op jit(solution)/shard_map/top_rows/pallas_call | solution.py:73
  3.2 9.5 %all-to-all-start = ((bf16[32,4,16,128]{3,2,1,0:T(8,128)(2,1)}), bf16[32,4,16,128]{3,2,1,0:T(8,128)(2,1)S(1)}, u32[]{:S(2)}, u32[]{:S(2)}) async-start(bf16[32,4,16,128]{3,2,1,0:T(8,128)(2,1)} %top_rows.1), calls=%async_computation | async-start | bytes 1048576 | tf_op jit(solution)/shard_map/all_to_all | solution.py:249
  12.7 0.1 pad_add_fusion.place
  12.8 1.7 %messages.1 = (bf16[640,128]{1,0:T(8,128)(2,1)S(1)}, bf16[640,128]{1,0:T(8,128)(2,1)S(1)}, bf16[640,128]{1,0:T(8,128)(2,1)S(1)}, bf16[640,128]{1,0:T(8,128)(2,1)S(1)}) custom-call(s32[2]{0:T(128)S(1)} %pad_add_fusion.place, s32[2,1,1,2]{3,2,1,0:T(1,128)S(1)} %bitcast.15, bf16[2,1,2,1,512,128]{5,4,3,2,1,0:T(8,128)(2,1)} %left_hbm.1, ...), custom_call_target="tpu_custom_call" | custom-call | flops 1000000 | bytes 1048576 | tf_op jit(solution)/shard_map/messages/pallas_call | solution.py:105
  14.5 3.3 %collective-permute-start = (bf16[640,128]{1,0:T(8,128)(2,1)S(1)}, bf16[640,128]{1,0:T(8,128)(2,1)S(1)}, u32[]{:S(2)}, u32[]{:S(2)}) collective-permute-start(bf16[640,128]{1,0:T(8,128)(2,1)S(1)} %get-tuple-element.12), channel_id=1, source_target_pairs={{0,2},{1,15},{16,18},{17,31},{32,34},{33,47},{48,50},{49,63},{64,6... | collective-permute-start | bytes 491528 | tf_op jit(solution)/shard_map/ppermute | solution.py:246
  17.9 8.2 %collective-permute-start.1 = (bf16[640,128]{1,0:T(8,128)(2,1)S(1)}, bf16[640,128]{1,0:T(8,128)(2,1)S(1)}, u32[]{:S(2)}, u32[]{:S(2)}) collective-permute-start(bf16[640,128]{1,0:T(8,128)(2,1)S(1)} %get-tuple-element.13), channel_id=1, source_target_pairs={{0,12},{1,5},{16,28},{17,21},{32,44},{33,37},{48,60},{49,53},{64,7... | collective-permute-start | bytes 491528 | tf_op jit(solution)/shard_map/ppermute | solution.py:247
  26.1 1.3 %collective-permute-start.2 = (bf16[640,128]{1,0:T(8,128)(2,1)S(1)}, bf16[640,128]{1,0:T(8,128)(2,1)S(1)}, u32[]{:S(2)}, u32[]{:S(2)}) collective-permute-start(bf16[640,128]{1,0:T(8,128)(2,1)S(1)} %get-tuple-element.14), channel_id=1, source_target_pairs={{0,6},{1,11},{16,22},{17,27},{32,38},{33,43},{48,54},{49,59},{64,7... | collective-permute-start | bytes 491528 | tf_op jit(solution)/shard_map/ppermute | solution.py:248
  27.4 0.0 all-to-all-done
  27.5 0.7 broadcast_in_dim.4
  28.1 9.1 %all-to-all-start.1 = ((bf16[16,32,128]{2,1,0:T(8,128)(2,1)}), bf16[16,32,128]{2,1,0:T(8,128)(2,1)S(1)}, u32[]{:S(2)}, u32[]{:S(2)}) async-start(bf16[16,32,128]{2,1,0:T(8,128)(2,1)} %broadcast_in_dim.4), calls=%async_computation.1 | async-start | bytes 262144 | tf_op jit(solution)/shard_map/all_to_all | solution.py:236
  37.3 0.0 collective-permute-done
  37.3 0.0 collective-permute-done.1
  37.3 0.0 collective-permute-done.2
  37.3 0.1 select_select_fusion
  37.4 5.9 %collective-permute-start.3 = (bf16[384,128]{1,0:T(8,128)(2,1)S(1)}, bf16[384,128]{1,0:T(8,128)(2,1)S(1)}, u32[]{:S(2)}, u32[]{:S(2)}) collective-permute-start(bf16[384,128]{1,0:T(8,128)(2,1)S(1)} %slice.55), channel_id=1, source_target_pairs={{0,14},{2,4},{6,8},{12,10},{1,3},{5,7},{11,9},{15,13},{16,30},{18,... | collective-permute-start | bytes 294920 | tf_op jit(solution)/shard_map/ppermute | solution.py:260
  43.3 3.1 %collective-permute-done.3 = bf16[384,128]{1,0:T(8,128)(2,1)S(1)} collective-permute-done((bf16[384,128]{1,0:T(8,128)(2,1)S(1)}, bf16[384,128]{1,0:T(8,128)(2,1)S(1)}, u32[]{:S(2)}, u32[]{:S(2)}) %collective-permute-start.3) | collective-permute-done | bytes 98336 | tf_op jit(solution)/shard_map/ppermute | solution.py:260
  46.4 5.2 %all-to-all-done.1 = bf16[16,32,128]{2,1,0:T(8,128)(2,1)S(1)} async-done(((bf16[16,32,128]{2,1,0:T(8,128)(2,1)}), bf16[16,32,128]{2,1,0:T(8,128)(2,1)S(1)}, u32[]{:S(2)}, u32[]{:S(2)}) %all-to-all-start.1) | async-done | bytes 131104 | tf_op jit(solution)/shard_map/all_to_all | solution.py:236
  51.7 1.5 %broadcast_in_dim.5 = bf16[32,192,128]{2,1,0:T(8,128)(2,1)} broadcast(bf16[192,128]{1,0:T(8,128)(2,1)S(1)} %pad_maximum_fusion), dimensions={1,2} | broadcast | bytes 1622016 | tf_op jit(solution)/shard_map/broadcast_in_dim | solution.py:235
  53.2 5.4 %all-to-all-start.2 = ((bf16[32,192,128]{2,1,0:T(8,128)(2,1)}), bf16[32,192,128]{2,1,0:T(8,128)(2,1)S(1)}, u32[]{:S(2)}, u32[]{:S(2)}) async-start(bf16[32,192,128]{2,1,0:T(8,128)(2,1)} %broadcast_in_dim.5), calls=%async_computation.2 | async-start | bytes 3145728 | tf_op jit(solution)/shard_map/all_to_all | solution.py:236
  58.6 3.4 %collective-permute-start.4 = (bf16[128,128]{1,0:T(8,128)(2,1)S(1)}, bf16[128,128]{1,0:T(8,128)(2,1)S(1)}, u32[]{:S(2)}, u32[]{:S(2)}) collective-permute-start(bf16[128,128]{1,0:T(8,128)(2,1)S(1)} %slice_select_fusion.1.mine), channel_id=1, source_target_pairs={{0,1},{1,0},{2,3},{3,2},{4,5},{5,4},{6,7},{7,6},{8,9},{9,8},{10,11... | collective-permute-start | bytes 98312 | tf_op jit(solution)/shard_map/ppermute | solution.py:263
  62.0 35.4 %all-gather = bf16[3840,128]{1,0:T(8,128)(2,1)} all-gather(bf16[240,128]{1,0:T(8,128)(2,1)S(1)} %slice_select_fusion), channel_id=2, replica_groups=mesh['row'=32,'col'=16] {'col'}, dimensions={0}, use_global_device_ids=true | all-gather | bytes 1044480 | tf_op jit(solution)/shard_map/all_gather | solution.py:268
  97.4 0.0 all-to-all-done.2
  97.4 7.6 %update_tiles.1 = bf16[2,1,2,1,512,512]{5,4,3,2,1,0:T(8,128)(2,1)} custom-call(s32[2]{0:T(128)S(1)} %pad_add_fusion.place, s32[2,1,1,2]{3,2,1,0:T(1,128)S(1)} %bitcast.16, bf16[2,1,2,1,512,128]{5,4,3,2,1,0:T(8,128)(2,1)} %left_hbm.1, bf16[2,1,2,1,512,128]{5,4,3,2,1,0:T(8,128)(2,1)} %right_hbm.1, bf16[16,240,128]{2,1,0:T(8,128)(2,1)} %bitcast.17, ...), custom_call_target="tpu_custom_call" | custom-call | flops 2500000000 | bytes 8388608 | tf_op jit(solution)/shard_map/update_tiles/pallas_call | solution.py:217
  (13 shorter events, 0.1 us)
Async XLA Ops:
  0.0 12.8 %copy-start.1 = (s32[2,1,2,1]{2,3,1,0:T(1,128)S(1)}, s32[2,1,2,1]{2,3,1,0:T(1,128)}, u32[]{:S(2)}) copy-start(s32[2,1,2,1]{2,3,1,0:T(1,128)} %param.6) | copy-start | bytes 52
  0.0 0.8 copy-start
  3.2 24.2 %all-to-all-start = ((bf16[32,4,16,128]{3,2,1,0:T(8,128)(2,1)}), bf16[32,4,16,128]{3,2,1,0:T(8,128)(2,1)S(1)}, u32[]{:S(2)}, u32[]{:S(2)}) async-start(bf16[32,4,16,128]{3,2,1,0:T(8,128)(2,1)} %top_rows.1), calls=%async_computation | async-start | bytes 1048576 | tf_op jit(solution)/shard_map/all_to_all | solution.py:249
  14.5 22.7 %collective-permute-start = (bf16[640,128]{1,0:T(8,128)(2,1)S(1)}, bf16[640,128]{1,0:T(8,128)(2,1)S(1)}, u32[]{:S(2)}, u32[]{:S(2)}) collective-permute-start(bf16[640,128]{1,0:T(8,128)(2,1)S(1)} %get-tuple-element.12), channel_id=1, source_target_pairs={{0,2},{1,15},{16,18},{17,31},{32,34},{33,47},{48,50},{49,63},{64,6... | collective-permute-start | bytes 491528 | tf_op jit(solution)/shard_map/ppermute | solution.py:246
  17.9 19.4 %collective-permute-start.1 = (bf16[640,128]{1,0:T(8,128)(2,1)S(1)}, bf16[640,128]{1,0:T(8,128)(2,1)S(1)}, u32[]{:S(2)}, u32[]{:S(2)}) collective-permute-start(bf16[640,128]{1,0:T(8,128)(2,1)S(1)} %get-tuple-element.13), channel_id=1, source_target_pairs={{0,12},{1,5},{16,28},{17,21},{32,44},{33,37},{48,60},{49,53},{64,7... | collective-permute-start | bytes 491528 | tf_op jit(solution)/shard_map/ppermute | solution.py:247
  26.1 11.2 %collective-permute-start.2 = (bf16[640,128]{1,0:T(8,128)(2,1)S(1)}, bf16[640,128]{1,0:T(8,128)(2,1)S(1)}, u32[]{:S(2)}, u32[]{:S(2)}) collective-permute-start(bf16[640,128]{1,0:T(8,128)(2,1)S(1)} %get-tuple-element.14), channel_id=1, source_target_pairs={{0,6},{1,11},{16,22},{17,27},{32,38},{33,43},{48,54},{49,59},{64,7... | collective-permute-start | bytes 491528 | tf_op jit(solution)/shard_map/ppermute | solution.py:248
  28.1 23.5 %all-to-all-start.1 = ((bf16[16,32,128]{2,1,0:T(8,128)(2,1)}), bf16[16,32,128]{2,1,0:T(8,128)(2,1)S(1)}, u32[]{:S(2)}, u32[]{:S(2)}) async-start(bf16[16,32,128]{2,1,0:T(8,128)(2,1)} %broadcast_in_dim.4), calls=%async_computation.1 | async-start | bytes 262144 | tf_op jit(solution)/shard_map/all_to_all | solution.py:236
  37.4 9.0 %collective-permute-start.3 = (bf16[384,128]{1,0:T(8,128)(2,1)S(1)}, bf16[384,128]{1,0:T(8,128)(2,1)S(1)}, u32[]{:S(2)}, u32[]{:S(2)}) collective-permute-start(bf16[384,128]{1,0:T(8,128)(2,1)S(1)} %slice.55), channel_id=1, source_target_pairs={{0,14},{2,4},{6,8},{12,10},{1,3},{5,7},{11,9},{15,13},{16,30},{18,... | collective-permute-start | bytes 294920 | tf_op jit(solution)/shard_map/ppermute | solution.py:260
  53.2 44.2 %all-to-all-start.2 = ((bf16[32,192,128]{2,1,0:T(8,128)(2,1)}), bf16[32,192,128]{2,1,0:T(8,128)(2,1)S(1)}, u32[]{:S(2)}, u32[]{:S(2)}) async-start(bf16[32,192,128]{2,1,0:T(8,128)(2,1)} %broadcast_in_dim.5), calls=%async_computation.2 | async-start | bytes 3145728 | tf_op jit(solution)/shard_map/all_to_all | solution.py:236
  58.6 38.8 %collective-permute-start.4 = (bf16[128,128]{1,0:T(8,128)(2,1)S(1)}, bf16[128,128]{1,0:T(8,128)(2,1)S(1)}, u32[]{:S(2)}, u32[]{:S(2)}) collective-permute-start(bf16[128,128]{1,0:T(8,128)(2,1)S(1)} %slice_select_fusion.1.mine), channel_id=1, source_target_pairs={{0,1},{1,0},{2,3},{3,2},{4,5},{5,4},{6,7},{7,6},{8,9},{9,8},{10,11... | collective-permute-start | bytes 98312 | tf_op jit(solution)/shard_map/ppermute | solution.py:263

commit v4 on v3

--- a/solution.py
+++ b/solution.py
@@ -11,6 +11,8 @@
 MAIN = 240
 REST = PIECE - MAIN
 HOLDERS = ((0, 14, 2, 4, 6, 8, 12, 10), (1, 3, 5, 7, 11, 9, 15, 13))
+OTHER_ONE = ((0, 1), (2, 3), (6, 7), (12, 13), (1, 0), (5, 6), (11, 10), (15, 14))
+OTHER_TWO = ((0, 15), (2, 5), (6, 9), (12, 11), (1, 2), (5, 4), (11, 8), (15, 12))
 VMEM = pl.BlockSpec(memory_space=pltpu.VMEM)
 SMEM = pl.BlockSpec(memory_space=pltpu.SMEM)
 HBM = pl.BlockSpec(memory_space=pltpu.HBM)
@@ -42,8 +44,8 @@
 
 
 def mask_rank(tile, rank):
-    column = lax.broadcasted_iota(jnp.int32, (512, 128), 1)
-    return jnp.where(column < rank, tile, jnp.zeros_like(tile))
+    column = lax.broadcasted_iota(jnp.int32, (1, 128), 1)
+    return tile * jnp.where(column < rank, 1.0, 0.0).astype(BF16)
 
 
 def in_hbm(*arrays):
@@ -60,12 +62,18 @@
     return copies
 
 
-def top_body(ranks, left, right, top, left_row, right_row, arrived):
-    pairs = ((left.at[0, 0, :, 0], left_row), (right.at[0, 0, :, 0], right_row))
-    for k, copy in enumerate(fetch(pairs, arrived)):
-        copy.wait()
+def top_body(ranks_hbm, left, right, top, ranks, left_row, right_row, arrived):
+    pairs = (
+        (ranks_hbm, ranks),
+        (left.at[0, 0, :, 0], left_row),
+        (right.at[0, 0, :, 0], right_row),
+    )
+    copies = fetch(pairs, arrived)
+    copies[0].wait()
+    for k in range(2):
+        copies[1 + k].wait()
         for b in range(2):
-            tile = mask_rank(pairs[k][1][b], ranks[0, 0, 0, b])
+            tile = mask_rank(pairs[1 + k][1][b], ranks[0, 0, 0, b])
             top[:, 2 * k + b] = tile.reshape(N_ROW, 16, 128)
 
 
@@ -73,13 +81,15 @@
     return pl.pallas_call(
         top_body,
         out_shape=jax.ShapeDtypeStruct((N_ROW, 4, 16, 128), BF16),
-        in_specs=[SMEM, HBM, HBM],
+        in_specs=[HBM] * 3,
         out_specs=VMEM,
-        scratch_shapes=[pltpu.VMEM((2, 512, 128), BF16)] * 2 + [pltpu.SemaphoreType.DMA((2,))],
+        scratch_shapes=[pltpu.SMEM((2, 1, 1, 2), jnp.int32)]
+        + [pltpu.VMEM((2, 512, 128), BF16)] * 2
+        + [pltpu.SemaphoreType.DMA((3,))],
         compiler_params=params(),
         cost_estimate=cost(10**6, 2**20),
         name="top_rows",
-    )(ranks, *in_hbm(left, right))
+    )(*in_hbm(ranks, left, right))
 
 
 def messages_body(
@@ -90,18 +100,22 @@
         copy.wait()
     tiles = [mask_rank(ref[a], ranks[a, 0, 0, 0]) for ref in (left_col, right_col) for a in range(2)]
     at_zero = place[1] == 0
-    own[:512] = tiles[0]
-    near[:512] = jnp.where(at_zero, tiles[1], tiles[3])
-    middle[:512] = jnp.where(at_zero, tiles[3], tiles[1])
-    far[:512] = tiles[2]
-    for k in range(8):
-        rest = tiles[k // 2][PIECE * (k % 2) + MAIN : PIECE * (k % 2 + 1)]
-        for message in (own, near, middle, far):
-            message[512 + REST * k : 512 + REST * (k + 1)] = rest
+    chosen = (
+        tiles[0],
+        jnp.where(at_zero, tiles[1], tiles[3]),
+        jnp.where(at_zero, tiles[3], tiles[1]),
+        tiles[2],
+    )
+    for message, tile in zip((own, near, middle, far), chosen):
+        message[:MAIN] = tile[:MAIN]
+        message[MAIN : 2 * MAIN] = tile[PIECE : PIECE + MAIN]
+        for k in range(8):
+            rest = tiles[k // 2][PIECE * (k % 2) + MAIN : PIECE * (k % 2 + 1)]
+            message[2 * MAIN + REST * k : 2 * MAIN + REST * (k + 1)] = rest
 
 
 def messages(place, ranks, left, right):
-    message = jax.ShapeDtypeStruct((512 + 8 * REST, 128), BF16)
+    message = jax.ShapeDtypeStruct((2 * MAIN + 8 * REST, 128), BF16)
     return pl.pallas_call(
         messages_body,
         out_shape=(message,) * 4,
@@ -128,13 +142,18 @@
     @pl.when(step == 0)
     def _():
         pairs = (
+            (inverses_hbm, inverses),
             (main_hbm, main),
-            (inverses_hbm, inverses),
             (left_hbm.at[:, 0, :, 0], left),
             (right_hbm.at[:, 0, :, 0], right),
         )
         copies = fetch(pairs, arrived)
         copies[0].wait()
+        lowers[:, 256:] = tn(inverses[0], row_tile(9)).astype(BF16)
+        pivot = tn(inverses[1], row_tile(11)).astype(BF16)
+        second[:, 128:256] = pivot
+        second[:, 384:] = pivot
+        ups[...] = jnp.concatenate([row_tile(0), row_tile(1), row_tile(10)], axis=1)
         copies[1].wait()
         even = q % 2 == 0
         rests = (
@@ -148,15 +167,12 @@
                 parts += [main[HOLDERS[panel][k]], rests[panel][REST * k : REST * (k + 1)]]
             return jnp.concatenate(parts, axis=0)
 
-        raw = jnp.concatenate([column_tile(0, 2), column_tile(0, 3), row_tile(9)], axis=1)
-        lowers[...] = tn(inverses[0], raw).astype(BF16)
-        ups[...] = jnp.concatenate([row_tile(0), row_tile(1), row_tile(10)], axis=1)
-        raw = jnp.concatenate([column_tile(1, 2), column_tile(1, 3), row_tile(11)], axis=1)
+        raw = jnp.concatenate([column_tile(0, 2), column_tile(0, 3)], axis=1)
+        lowers[:, :256] = tn(inverses[0], raw).astype(BF16)
+        raw = jnp.concatenate([column_tile(1, 2), column_tile(1, 3)], axis=1)
         fresh = tn(inverses[1], raw).astype(BF16)
         second[:, :128] = fresh[:, :128]
-        second[:, 128:256] = fresh[:, 256:]
-        second[:, 256:384] = fresh[:, 128:256]
-        second[:, 384:] = fresh[:, 256:]
+        second[:, 256:384] = fresh[:, 128:]
 
         line = lax.broadcasted_iota(jnp.int32, (384, 384), 0)
         column = lax.broadcasted_iota(jnp.int32, (384, 384), 1)
@@ -257,9 +273,9 @@
     is_head = (q < 2) | by_near | by_middle | (q == 6) | (q == 11)
     head = jnp.where(q < 2, own, jnp.where(by_near, near, jnp.where(by_middle, middle, far)))
     hops = [(line[k], line[k + 1]) for line in HOLDERS for k in range(0, 8, 2)]
-    moved = lax.ppermute(head[PIECE:], "col", hops)
+    moved = lax.ppermute(head[MAIN:], "col", hops)
     piece = jnp.where(is_head, head[:MAIN], moved[:MAIN])
-    mine = jnp.where(is_head, head[512:], moved[PIECE:])
+    mine = jnp.where(is_head, head[2 * MAIN :], moved[MAIN:])
     other = lax.ppermute(mine, "col", [(i, i ^ 1) for i in range(N_COL)])
 
     block = jnp.concatenate([scattered.reshape(128, 128), corner], axis=0)

time: 106 us -> 104 us (0.981)
  no operation moved by 1% of the time
where the time goes in v4:
time: 104 us
  starting transfers between devices  46.1 us (44%)
  blocking collectives  35.4 us (34%)
  Pallas kernels  11.2 us (11%)
  waiting for transfers between devices  8.31 us (8%)
  local copies, waits for them, and re-layouts  2.19 us (2%)
    all_gather x1, blocking collectives, per_device(): main = lax.all_gather(piece, 'col')  35.4 us
    all_to_all x2, starting transfers between devices, to_all(): return lax.all_to_all(sent, axis, 0, 0, tiled=True)  14.6 us
    all_to_all x1, starting transfers between devices, per_device(): scattered = lax.all_to_all(top, 'row', 0, 0, tiled=True)[:2]  9.47 us
    ppermute x1, starting transfers between devices, per_device(): middle = lax.ppermute(middle, 'col', [(0, 12), (1, 5)])  8.23 us
    pallas_call x1, Pallas kernels, update_tiles(): pl.pallas_call(update_body, grid=(4,), out_shape=jax.ShapeDtypeStruct((2,...  7.59 us
    ppermute x1, starting transfers between devices, per_device(): moved = lax.ppermute(head[MAIN:], 'col', hops)  5.95 us
    all_to_all x2, waiting for transfers between devices, to_all(): return lax.all_to_all(sent, axis, 0, 0, tiled=True)  5.32 us
    ppermute x1, starting transfers between devices, per_device(): near = lax.ppermute(near, 'col', [(0, 2), (1, 15)])  3.35 us
  transfers between devices with their start and end apart: 8, of which 2 were waited for; matrix products, arithmetic and copies ran while one was open for 1% of the time, Pallas kernels for 2%

profile of v4, /device:TPU:2, one launch (start us, length us, event | category | flops | bytes accessed | tf_op | source)
XLA Modules:
  0.0 103.6 jit_solution(3666292668288358816)
XLA Ops:
  0.0 1.9 %top_rows.1 = bf16[32,4,16,128]{3,2,1,0:T(8,128)(2,1)} custom-call(s32[2,1,1,2]{3,2,1,0:T(1,128)} %bitcast.14, bf16[2,1,2,1,512,128]{5,4,3,2,1,0:T(8,128)(2,1)} %left_hbm.1, bf16[2,1,2,1,512,128]{5,4,3,2,1,0:T(8,128)(2,1)} %right_hbm.1), custom_call_target="tpu_custom_call" | custom-call | flops 1000000 | bytes 1048576 | tf_op jit(solution)/shard_map/top_rows/pallas_call | solution.py:81
  1.9 9.5 %all-to-all-start = ((bf16[32,4,16,128]{3,2,1,0:T(8,128)(2,1)}), bf16[32,4,16,128]{3,2,1,0:T(8,128)(2,1)S(1)}, u32[]{:S(2)}, u32[]{:S(2)}) async-start(bf16[32,4,16,128]{3,2,1,0:T(8,128)(2,1)} %top_rows.1), calls=%async_computation | async-start | bytes 1048576 | tf_op jit(solution)/shard_map/all_to_all | solution.py:265
  11.4 0.1 pad_add_fusion.place
  11.5 1.7 %messages.1 = (bf16[608,128]{1,0:T(8,128)(2,1)S(1)}, bf16[608,128]{1,0:T(8,128)(2,1)S(1)}, bf16[608,128]{1,0:T(8,128)(2,1)S(1)}, bf16[608,128]{1,0:T(8,128)(2,1)S(1)}) custom-call(s32[2]{0:T(128)S(1)} %pad_add_fusion.place, s32[2,1,1,2]{3,2,1,0:T(1,128)S(1)} %bitcast.15, bf16[2,1,2,1,512,128]{5,4,3,2,1,0:T(8,128)(2,1)} %left_hbm.1, ...), custom_call_target="tpu_custom_call" | custom-call | flops 1000000 | bytes 1048576 | tf_op jit(solution)/shard_map/messages/pallas_call | solution.py:119
  13.2 3.3 %collective-permute-start = (bf16[608,128]{1,0:T(8,128)(2,1)S(1)}, bf16[608,128]{1,0:T(8,128)(2,1)S(1)}, u32[]{:S(2)}, u32[]{:S(2)}) collective-permute-start(bf16[608,128]{1,0:T(8,128)(2,1)S(1)} %get-tuple-element.12), channel_id=1, source_target_pairs={{0,2},{1,15},{16,18},{17,31},{32,34},{33,47},{48,50},{49,63},{64,6... | collective-permute-start | bytes 466952 | tf_op jit(solution)/shard_map/ppermute | solution.py:262
  16.5 8.2 %collective-permute-start.1 = (bf16[608,128]{1,0:T(8,128)(2,1)S(1)}, bf16[608,128]{1,0:T(8,128)(2,1)S(1)}, u32[]{:S(2)}, u32[]{:S(2)}) collective-permute-start(bf16[608,128]{1,0:T(8,128)(2,1)S(1)} %get-tuple-element.13), channel_id=1, source_target_pairs={{0,12},{1,5},{16,28},{17,21},{32,44},{33,37},{48,60},{49,53},{64,7... | collective-permute-start | bytes 466952 | tf_op jit(solution)/shard_map/ppermute | solution.py:263
  24.8 1.3 %collective-permute-start.2 = (bf16[608,128]{1,0:T(8,128)(2,1)S(1)}, bf16[608,128]{1,0:T(8,128)(2,1)S(1)}, u32[]{:S(2)}, u32[]{:S(2)}) collective-permute-start(bf16[608,128]{1,0:T(8,128)(2,1)S(1)} %get-tuple-element.14), channel_id=1, source_target_pairs={{0,6},{1,11},{16,22},{17,27},{32,38},{33,43},{48,54},{49,59},{64,7... | collective-permute-start | bytes 466952 | tf_op jit(solution)/shard_map/ppermute | solution.py:264
  26.1 0.0 all-to-all-done
  26.1 0.7 broadcast_in_dim.4
  26.8 9.2 %all-to-all-start.1 = ((bf16[16,32,128]{2,1,0:T(8,128)(2,1)}), bf16[16,32,128]{2,1,0:T(8,128)(2,1)S(1)}, u32[]{:S(2)}, u32[]{:S(2)}) async-start(bf16[16,32,128]{2,1,0:T(8,128)(2,1)} %broadcast_in_dim.4), calls=%async_computation.1 | async-start | bytes 262144 | tf_op jit(solution)/shard_map/all_to_all | solution.py:252
  36.0 0.0 collective-permute-done
  36.0 0.0 collective-permute-done.1
  36.0 0.0 collective-permute-done.2
  36.0 0.1 select_select_fusion
  36.1 5.9 %collective-permute-start.3 = (bf16[368,128]{1,0:T(8,128)(2,1)S(1)}, bf16[368,128]{1,0:T(8,128)(2,1)S(1)}, u32[]{:S(2)}, u32[]{:S(2)}) collective-permute-start(bf16[368,128]{1,0:T(8,128)(2,1)S(1)} %slice.55), channel_id=1, source_target_pairs={{0,14},{2,4},{6,8},{12,10},{1,3},{5,7},{11,9},{15,13},{16,30},{18,... | collective-permute-start | bytes 282632 | tf_op jit(solution)/shard_map/ppermute | solution.py:276
  42.0 3.0 %collective-permute-done.3 = bf16[368,128]{1,0:T(8,128)(2,1)S(1)} collective-permute-done((bf16[368,128]{1,0:T(8,128)(2,1)S(1)}, bf16[368,128]{1,0:T(8,128)(2,1)S(1)}, u32[]{:S(2)}, u32[]{:S(2)}) %collective-permute-start.3) | collective-permute-done | bytes 94240 | tf_op jit(solution)/shard_map/ppermute | solution.py:276
  45.0 5.3 %all-to-all-done.1 = bf16[16,32,128]{2,1,0:T(8,128)(2,1)S(1)} async-done(((bf16[16,32,128]{2,1,0:T(8,128)(2,1)}), bf16[16,32,128]{2,1,0:T(8,128)(2,1)S(1)}, u32[]{:S(2)}, u32[]{:S(2)}) %all-to-all-start.1) | async-done | bytes 131104 | tf_op jit(solution)/shard_map/all_to_all | solution.py:252
  50.4 1.5 %broadcast_in_dim.5 = bf16[32,192,128]{2,1,0:T(8,128)(2,1)} broadcast(bf16[192,128]{1,0:T(8,128)(2,1)S(1)} %pad_maximum_fusion), dimensions={1,2} | broadcast | bytes 1622016 | tf_op jit(solution)/shard_map/broadcast_in_dim | solution.py:251
  51.9 5.4 %all-to-all-start.2 = ((bf16[32,192,128]{2,1,0:T(8,128)(2,1)}), bf16[32,192,128]{2,1,0:T(8,128)(2,1)S(1)}, u32[]{:S(2)}, u32[]{:S(2)}) async-start(bf16[32,192,128]{2,1,0:T(8,128)(2,1)} %broadcast_in_dim.5), calls=%async_computation.2 | async-start | bytes 3145728 | tf_op jit(solution)/shard_map/all_to_all | solution.py:252
  57.3 3.3 %collective-permute-start.4 = (bf16[128,128]{1,0:T(8,128)(2,1)S(1)}, bf16[128,128]{1,0:T(8,128)(2,1)S(1)}, u32[]{:S(2)}, u32[]{:S(2)}) collective-permute-start(bf16[128,128]{1,0:T(8,128)(2,1)S(1)} %slice_select_fusion.1.mine), channel_id=1, source_target_pairs={{0,1},{1,0},{2,3},{3,2},{4,5},{5,4},{6,7},{7,6},{8,9},{9,8},{10,11... | collective-permute-start | bytes 98312 | tf_op jit(solution)/shard_map/ppermute | solution.py:279
  60.6 35.4 %all-gather = bf16[3840,128]{1,0:T(8,128)(2,1)} all-gather(bf16[240,128]{1,0:T(8,128)(2,1)S(1)} %slice_select_fusion), channel_id=2, replica_groups=mesh['row'=32,'col'=16] {'col'}, dimensions={0}, use_global_device_ids=true | all-gather | bytes 1044480 | tf_op jit(solution)/shard_map/all_gather | solution.py:284
  96.0 0.0 collective-permute-done.4.other
  96.0 0.0 all-to-all-done.2
  96.0 7.6 %update_tiles.1 = bf16[2,1,2,1,512,512]{5,4,3,2,1,0:T(8,128)(2,1)} custom-call(s32[2]{0:T(128)S(1)} %pad_add_fusion.place, s32[2,1,1,2]{3,2,1,0:T(1,128)S(1)} %bitcast.16, bf16[2,1,2,1,512,128]{5,4,3,2,1,0:T(8,128)(2,1)} %left_hbm.1, bf16[2,1,2,1,512,128]{5,4,3,2,1,0:T(8,128)(2,1)} %right_hbm.1, bf16[16,240,128]{2,1,0:T(8,128)(2,1)} %bitcast.17, ...), custom_call_target="tpu_custom_call" | custom-call | flops 2500000000 | bytes 8388608 | tf_op jit(solution)/shard_map/update_tiles/pallas_call | solution.py:233
  (11 shorter events, 0.1 us)
Async XLA Ops:
  0.0 11.5 %copy-start = (s32[2,1,2,1]{2,3,1,0:T(1,128)S(1)}, s32[2,1,2,1]{2,3,1,0:T(1,128)}, u32[]{:S(2)}) copy-start(s32[2,1,2,1]{2,3,1,0:T(1,128)} %param.6) | copy-start | bytes 52
  1.9 24.2 %all-to-all-start = ((bf16[32,4,16,128]{3,2,1,0:T(8,128)(2,1)}), bf16[32,4,16,128]{3,2,1,0:T(8,128)(2,1)S(1)}, u32[]{:S(2)}, u32[]{:S(2)}) async-start(bf16[32,4,16,128]{3,2,1,0:T(8,128)(2,1)} %top_rows.1), calls=%async_computation | async-start | bytes 1048576 | tf_op jit(solution)/shard_map/all_to_all | solution.py:265
  13.2 22.8 %collective-permute-start = (bf16[608,128]{1,0:T(8,128)(2,1)S(1)}, bf16[608,128]{1,0:T(8,128)(2,1)S(1)}, u32[]{:S(2)}, u32[]{:S(2)}) collective-permute-start(bf16[608,128]{1,0:T(8,128)(2,1)S(1)} %get-tuple-element.12), channel_id=1, source_target_pairs={{0,2},{1,15},{16,18},{17,31},{32,34},{33,47},{48,50},{49,63},{64,6... | collective-permute-start | bytes 466952 | tf_op jit(solution)/shard_map/ppermute | solution.py:262
  16.5 19.5 %collective-permute-start.1 = (bf16[608,128]{1,0:T(8,128)(2,1)S(1)}, bf16[608,128]{1,0:T(8,128)(2,1)S(1)}, u32[]{:S(2)}, u32[]{:S(2)}) collective-permute-start(bf16[608,128]{1,0:T(8,128)(2,1)S(1)} %get-tuple-element.13), channel_id=1, source_target_pairs={{0,12},{1,5},{16,28},{17,21},{32,44},{33,37},{48,60},{49,53},{64,7... | collective-permute-start | bytes 466952 | tf_op jit(solution)/shard_map/ppermute | solution.py:263
  24.8 11.2 %collective-permute-start.2 = (bf16[608,128]{1,0:T(8,128)(2,1)S(1)}, bf16[608,128]{1,0:T(8,128)(2,1)S(1)}, u32[]{:S(2)}, u32[]{:S(2)}) collective-permute-start(bf16[608,128]{1,0:T(8,128)(2,1)S(1)} %get-tuple-element.14), channel_id=1, source_target_pairs={{0,6},{1,11},{16,22},{17,27},{32,38},{33,43},{48,54},{49,59},{64,7... | collective-permute-start | bytes 466952 | tf_op jit(solution)/shard_map/ppermute | solution.py:264
  26.8 23.6 %all-to-all-start.1 = ((bf16[16,32,128]{2,1,0:T(8,128)(2,1)}), bf16[16,32,128]{2,1,0:T(8,128)(2,1)S(1)}, u32[]{:S(2)}, u32[]{:S(2)}) async-start(bf16[16,32,128]{2,1,0:T(8,128)(2,1)} %broadcast_in_dim.4), calls=%async_computation.1 | async-start | bytes 262144 | tf_op jit(solution)/shard_map/all_to_all | solution.py:252
  36.1 9.0 %collective-permute-start.3 = (bf16[368,128]{1,0:T(8,128)(2,1)S(1)}, bf16[368,128]{1,0:T(8,128)(2,1)S(1)}, u32[]{:S(2)}, u32[]{:S(2)}) collective-permute-start(bf16[368,128]{1,0:T(8,128)(2,1)S(1)} %slice.55), channel_id=1, source_target_pairs={{0,14},{2,4},{6,8},{12,10},{1,3},{5,7},{11,9},{15,13},{16,30},{18,... | collective-permute-start | bytes 282632 | tf_op jit(solution)/shard_map/ppermute | solution.py:276
  51.9 44.1 %all-to-all-start.2 = ((bf16[32,192,128]{2,1,0:T(8,128)(2,1)}), bf16[32,192,128]{2,1,0:T(8,128)(2,1)S(1)}, u32[]{:S(2)}, u32[]{:S(2)}) async-start(bf16[32,192,128]{2,1,0:T(8,128)(2,1)} %broadcast_in_dim.5), calls=%async_computation.2 | async-start | bytes 3145728 | tf_op jit(solution)/shard_map/all_to_all | solution.py:252
  57.3 38.7 %collective-permute-start.4 = (bf16[128,128]{1,0:T(8,128)(2,1)S(1)}, bf16[128,128]{1,0:T(8,128)(2,1)S(1)}, u32[]{:S(2)}, u32[]{:S(2)}) collective-permute-start(bf16[128,128]{1,0:T(8,128)(2,1)S(1)} %slice_select_fusion.1.mine), channel_id=1, source_target_pairs={{0,1},{1,0},{2,3},{3,2},{4,5},{5,4},{6,7},{7,6},{8,9},{9,8},{10,11... | collective-permute-start | bytes 98312 | tf_op jit(solution)/shard_map/ppermute | solution.py:279

commit v5 on v4

--- a/solution.py
+++ b/solution.py
@@ -62,19 +62,16 @@
     return copies
 
 
-def top_body(ranks_hbm, left, right, top, ranks, left_row, right_row, arrived):
-    pairs = (
-        (ranks_hbm, ranks),
-        (left.at[0, 0, :, 0], left_row),
-        (right.at[0, 0, :, 0], right_row),
-    )
+def top_body(ranks_hbm, left, right, top, ranks, tiles, arrived):
+    pairs = [(ranks_hbm, ranks)]
+    for t in range(4):
+        source = (left, right)[t // 2]
+        pairs.append((source.at[0, 0, t % 2, 0], tiles.at[t]))
     copies = fetch(pairs, arrived)
     copies[0].wait()
-    for k in range(2):
-        copies[1 + k].wait()
-        for b in range(2):
-            tile = mask_rank(pairs[1 + k][1][b], ranks[0, 0, 0, b])
-            top[:, 2 * k + b] = tile.reshape(N_ROW, 16, 128)
+    for t in range(4):
+        copies[1 + t].wait()
+        top[:, t] = mask_rank(tiles[t], ranks[0, 0, 0, t % 2]).reshape(N_ROW, 16, 128)
 
 
 def top_rows(ranks, left, right):
@@ -84,8 +81,7 @@
         in_specs=[HBM] * 3,
         out_specs=VMEM,
         scratch_shapes=[pltpu.SMEM((2, 1, 1, 2), jnp.int32)]
-        + [pltpu.VMEM((2, 512, 128), BF16)] * 2
-        + [pltpu.SemaphoreType.DMA((3,))],
+        + [pltpu.VMEM((4, 512, 128), BF16), pltpu.SemaphoreType.DMA((5,))],
         compiler_params=params(),
         cost_estimate=cost(10**6, 2**20),
         name="top_rows",
@@ -129,8 +125,8 @@
 
 
 def update_body(
-    place, ranks, left_hbm, right_hbm, main_hbm, inverses_hbm, mine, other, rows, out,
-    left, right, main, inverses, arrived, lowers, ups, second, wide, tall, upper, update, change,
+    place, ranks, left_hbm, right_hbm, inverses_hbm, main, mine, other, rows, out,
+    left, right, inverses, arrived, lowers, ups, second, wide, tall, upper, update, change,
 ):
     p, q = place[0], place[1]
     step = pl.program_id(0)
@@ -143,18 +139,20 @@
     def _():
         pairs = (
             (inverses_hbm, inverses),
-            (main_hbm, main),
             (left_hbm.at[:, 0, :, 0], left),
             (right_hbm.at[:, 0, :, 0], right),
         )
         copies = fetch(pairs, arrived)
+        ups[...] = jnp.concatenate([row_tile(0), row_tile(1), row_tile(10)], axis=1)
+        for k in range(2):
+            wide[:, 256 * k : 256 * k + 128] = row_tile(4 + k)
+            upper[k, :, :128] = row_tile(6 + k)
+            upper[k, :, 128:] = row_tile(2 + k)
         copies[0].wait()
         lowers[:, 256:] = tn(inverses[0], row_tile(9)).astype(BF16)
         pivot = tn(inverses[1], row_tile(11)).astype(BF16)
         second[:, 128:256] = pivot
         second[:, 384:] = pivot
-        ups[...] = jnp.concatenate([row_tile(0), row_tile(1), row_tile(10)], axis=1)
-        copies[1].wait()
         even = q % 2 == 0
         rests = (
             jnp.where(even, mine[...], other[...]),
@@ -184,11 +182,8 @@
             update[k] = result.astype(BF16)
             tall[k, :, :128] = column_tile(1, k)
             tall[k, :, 128:] = update[k, :, 256:]
-            upper[k, :, :128] = row_tile(6 + k)
-            upper[k, :, 128:] = row_tile(2 + k)
         result = -nn(row_tile(8), inner[256:, :256])
         for k in range(2):
-            wide[:, 256 * k : 256 * k + 128] = row_tile(4 + k)
             wide[:, 256 * k + 128 : 256 * k + 256] = result[:, 128 * k : 128 * (k + 1)].astype(BF16)
 
         line = lax.broadcasted_iota(jnp.int32, (512, 512), 0)
@@ -200,8 +195,8 @@
             result = -nn(tall[k], inner[256 * k : 256 * (k + 1)])
             for j in range(2):
                 change[k, j] = result[:, 256 * j : 256 * (j + 1)].astype(BF16)
+        copies[1].wait()
         copies[2].wait()
-        copies[3].wait()
 
     row = a * N_ROW + p
     col = b * N_COL + q
@@ -234,17 +229,17 @@
         update_body,
         grid=(4,),
         out_shape=jax.ShapeDtypeStruct((2, 1, 2, 1, 512, 512), BF16),
-        in_specs=[SMEM, SMEM] + [HBM] * 4 + [VMEM] * 3,
+        in_specs=[SMEM, SMEM] + [HBM] * 3 + [VMEM] * 4,
         out_specs=pl.BlockSpec(
             (1, 1, 1, 1, 512, 512), lambda s: (s // 2, 0, s % 2, 0, 0, 0)
         ),
-        scratch_shapes=[four, four, pltpu.VMEM((N_COL, MAIN, 128), BF16)]
+        scratch_shapes=[four, four]
         + [pltpu.VMEM((2, 512, 512), BF16), pltpu.SemaphoreType.DMA((4,))]
         + [pltpu.VMEM(shape, BF16) for shape in shapes],
         compiler_params=params(),
         cost_estimate=cost(25 * 10**8, 8 * 2**20),
         name="update_tiles",
-    )(place, ranks, *in_hbm(left, right, main, inverses), mine, other, rows)
+    )(place, ranks, *in_hbm(left, right, inverses), main, mine, other, rows)
 
 
 def to_all(block, axis, size):

time: 104 us -> 102 us (0.981)
  blocking collectives: 35.4 us -> 33.3 us
    all_gather x1, blocking collectives: 35.4 us -> 33.3 us  [per_device(): main = lax.all_gather(piece, 'col')]
where the time goes in v5:
time: 102 us; the launch traced here: 101 us
  starting transfers between devices  46.1 us (45%)
  blocking collectives  33.3 us (33%)
  Pallas kernels  10.8 us (11%)
  waiting for transfers between devices  8.31 us (8%)
  local copies, waits for them, and re-layouts  2.19 us (2%)
    all_gather x1, blocking collectives, per_device(): main = lax.all_gather(piece, 'col')  33.3 us
    all_to_all x2, starting transfers between devices, to_all(): return lax.all_to_all(sent, axis, 0, 0, tiled=True)  14.6 us
    all_to_all x1, starting transfers between devices, per_device(): scattered = lax.all_to_all(top, 'row', 0, 0, tiled=True)[:2]  9.47 us
    ppermute x1, starting transfers between devices, per_device(): middle = lax.ppermute(middle, 'col', [(0, 12), (1, 5)])  8.23 us
    pallas_call x1, Pallas kernels, update_tiles(): pl.pallas_call(update_body, grid=(4,), out_shape=jax.ShapeDtypeStruct((2,...  7.18 us
    ppermute x1, starting transfers between devices, per_device(): moved = lax.ppermute(head[MAIN:], 'col', hops)  5.95 us
    all_to_all x2, waiting for transfers between devices, to_all(): return lax.all_to_all(sent, axis, 0, 0, tiled=True)  5.32 us
    ppermute x1, starting transfers between devices, per_device(): near = lax.ppermute(near, 'col', [(0, 2), (1, 15)])  3.35 us
  transfers between devices with their start and end apart: 8, of which 2 were waited for; matrix products, arithmetic and copies ran while one was open for 1% of the time, Pallas kernels for 2%

profile of v5, /device:TPU:2, one launch (start us, length us, event | category | flops | bytes accessed | tf_op | source)
XLA Modules:
  0.0 101.2 jit_solution(15182375181529648014)
XLA Ops:
  0.0 2.0 %top_rows.1 = bf16[32,4,16,128]{3,2,1,0:T(8,128)(2,1)} custom-call(s32[2,1,1,2]{3,2,1,0:T(1,128)} %bitcast.15, bf16[2,1,2,1,512,128]{5,4,3,2,1,0:T(8,128)(2,1)} %left_hbm.1, bf16[2,1,2,1,512,128]{5,4,3,2,1,0:T(8,128)(2,1)} %right_hbm.1), custom_call_target="tpu_custom_call" | custom-call | flops 1000000 | bytes 1048576 | tf_op jit(solution)/shard_map/top_rows/pallas_call | solution.py:78
  2.0 9.5 %all-to-all-start = ((bf16[32,4,16,128]{3,2,1,0:T(8,128)(2,1)}), bf16[32,4,16,128]{3,2,1,0:T(8,128)(2,1)S(1)}, u32[]{:S(2)}, u32[]{:S(2)}) async-start(bf16[32,4,16,128]{3,2,1,0:T(8,128)(2,1)} %top_rows.1), calls=%async_computation | async-start | bytes 1048576 | tf_op jit(solution)/shard_map/all_to_all | solution.py:260
  11.5 0.1 pad_add_fusion.place
  11.5 1.7 %messages.1 = (bf16[608,128]{1,0:T(8,128)(2,1)S(1)}, bf16[608,128]{1,0:T(8,128)(2,1)S(1)}, bf16[608,128]{1,0:T(8,128)(2,1)S(1)}, bf16[608,128]{1,0:T(8,128)(2,1)S(1)}) custom-call(s32[2]{0:T(128)S(1)} %pad_add_fusion.place, s32[2,1,1,2]{3,2,1,0:T(1,128)S(1)} %bitcast.16, bf16[2,1,2,1,512,128]{5,4,3,2,1,0:T(8,128)(2,1)} %left_hbm.1, ...), custom_call_target="tpu_custom_call" | custom-call | flops 1000000 | bytes 1048576 | tf_op jit(solution)/shard_map/messages/pallas_call | solution.py:115
  13.2 3.3 %collective-permute-start = (bf16[608,128]{1,0:T(8,128)(2,1)S(1)}, bf16[608,128]{1,0:T(8,128)(2,1)S(1)}, u32[]{:S(2)}, u32[]{:S(2)}) collective-permute-start(bf16[608,128]{1,0:T(8,128)(2,1)S(1)} %get-tuple-element.12), channel_id=1, source_target_pairs={{0,2},{1,15},{16,18},{17,31},{32,34},{33,47},{48,50},{49,63},{64,6... | collective-permute-start | bytes 466952 | tf_op jit(solution)/shard_map/ppermute | solution.py:257
  16.6 8.2 %collective-permute-start.1 = (bf16[608,128]{1,0:T(8,128)(2,1)S(1)}, bf16[608,128]{1,0:T(8,128)(2,1)S(1)}, u32[]{:S(2)}, u32[]{:S(2)}) collective-permute-start(bf16[608,128]{1,0:T(8,128)(2,1)S(1)} %get-tuple-element.13), channel_id=1, source_target_pairs={{0,12},{1,5},{16,28},{17,21},{32,44},{33,37},{48,60},{49,53},{64,7... | collective-permute-start | bytes 466952 | tf_op jit(solution)/shard_map/ppermute | solution.py:258
  24.8 1.3 %collective-permute-start.2 = (bf16[608,128]{1,0:T(8,128)(2,1)S(1)}, bf16[608,128]{1,0:T(8,128)(2,1)S(1)}, u32[]{:S(2)}, u32[]{:S(2)}) collective-permute-start(bf16[608,128]{1,0:T(8,128)(2,1)S(1)} %get-tuple-element.14), channel_id=1, source_target_pairs={{0,6},{1,11},{16,22},{17,27},{32,38},{33,43},{48,54},{49,59},{64,7... | collective-permute-start | bytes 466952 | tf_op jit(solution)/shard_map/ppermute | solution.py:259
  26.1 0.0 all-to-all-done
  26.2 0.7 broadcast_in_dim.4
  26.9 9.2 %all-to-all-start.1 = ((bf16[16,32,128]{2,1,0:T(8,128)(2,1)}), bf16[16,32,128]{2,1,0:T(8,128)(2,1)S(1)}, u32[]{:S(2)}, u32[]{:S(2)}) async-start(bf16[16,32,128]{2,1,0:T(8,128)(2,1)} %broadcast_in_dim.4), calls=%async_computation.1 | async-start | bytes 262144 | tf_op jit(solution)/shard_map/all_to_all | solution.py:247
  36.0 0.0 collective-permute-done
  36.0 0.0 collective-permute-done.1
  36.0 0.0 collective-permute-done.2
  36.1 0.1 select_select_fusion
  36.1 5.9 %collective-permute-start.3 = (bf16[368,128]{1,0:T(8,128)(2,1)S(1)}, bf16[368,128]{1,0:T(8,128)(2,1)S(1)}, u32[]{:S(2)}, u32[]{:S(2)}) collective-permute-start(bf16[368,128]{1,0:T(8,128)(2,1)S(1)} %slice.55), channel_id=1, source_target_pairs={{0,14},{2,4},{6,8},{12,10},{1,3},{5,7},{11,9},{15,13},{16,30},{18,... | collective-permute-start | bytes 282632 | tf_op jit(solution)/shard_map/ppermute | solution.py:271
  42.1 3.0 %collective-permute-done.3 = bf16[368,128]{1,0:T(8,128)(2,1)S(1)} collective-permute-done((bf16[368,128]{1,0:T(8,128)(2,1)S(1)}, bf16[368,128]{1,0:T(8,128)(2,1)S(1)}, u32[]{:S(2)}, u32[]{:S(2)}) %collective-permute-start.3) | collective-permute-done | bytes 94240 | tf_op jit(solution)/shard_map/ppermute | solution.py:271
  45.1 5.3 %all-to-all-done.1 = bf16[16,32,128]{2,1,0:T(8,128)(2,1)S(1)} async-done(((bf16[16,32,128]{2,1,0:T(8,128)(2,1)}), bf16[16,32,128]{2,1,0:T(8,128)(2,1)S(1)}, u32[]{:S(2)}, u32[]{:S(2)}) %all-to-all-start.1) | async-done | bytes 131104 | tf_op jit(solution)/shard_map/all_to_all | solution.py:247
  50.4 1.5 %broadcast_in_dim.5 = bf16[32,192,128]{2,1,0:T(8,128)(2,1)} broadcast(bf16[192,128]{1,0:T(8,128)(2,1)S(1)} %pad_maximum_fusion), dimensions={1,2} | broadcast | bytes 1622016 | tf_op jit(solution)/shard_map/broadcast_in_dim | solution.py:246
  51.9 5.4 %all-to-all-start.2 = ((bf16[32,192,128]{2,1,0:T(8,128)(2,1)}), bf16[32,192,128]{2,1,0:T(8,128)(2,1)S(1)}, u32[]{:S(2)}, u32[]{:S(2)}) async-start(bf16[32,192,128]{2,1,0:T(8,128)(2,1)} %broadcast_in_dim.5), calls=%async_computation.2 | async-start | bytes 3145728 | tf_op jit(solution)/shard_map/all_to_all | solution.py:247
  57.4 3.3 %collective-permute-start.4 = (bf16[128,128]{1,0:T(8,128)(2,1)S(1)}, bf16[128,128]{1,0:T(8,128)(2,1)S(1)}, u32[]{:S(2)}, u32[]{:S(2)}) collective-permute-start(bf16[128,128]{1,0:T(8,128)(2,1)S(1)} %slice_select_fusion.1.mine), channel_id=1, source_target_pairs={{0,1},{1,0},{2,3},{3,2},{4,5},{5,4},{6,7},{7,6},{8,9},{9,8},{10,11... | collective-permute-start | bytes 98312 | tf_op jit(solution)/shard_map/ppermute | solution.py:274
  60.6 33.3 %all-gather = bf16[3840,128]{1,0:T(8,128)(2,1)S(1)} all-gather(bf16[240,128]{1,0:T(8,128)(2,1)S(1)} %slice_select_fusion), channel_id=2, replica_groups=mesh['row'=32,'col'=16] {'col'}, dimensions={0}, use_global_device_ids=true | all-gather | bytes 1044480 | tf_op jit(solution)/shard_map/all_gather | solution.py:279
  94.0 0.0 collective-permute-done.4.other
  94.0 0.0 all-to-all-done.2
  94.0 7.2 %update_tiles.1 = bf16[2,1,2,1,512,512]{5,4,3,2,1,0:T(8,128)(2,1)} custom-call(s32[2]{0:T(128)S(1)} %pad_add_fusion.place, s32[2,1,1,2]{3,2,1,0:T(1,128)S(1)} %bitcast.17, bf16[2,1,2,1,512,128]{5,4,3,2,1,0:T(8,128)(2,1)} %left_hbm.1, bf16[2,1,2,1,512,128]{5,4,3,2,1,0:T(8,128)(2,1)} %right_hbm.1, bf16[2,512,512]{2,1,0:T(8,128)(2,1)} %inverses_hbm.1, ...), custom_call_target="tpu_custom_call" | custom-call | flops 2500000000 | bytes 8388608 | tf_op jit(solution)/shard_map/update_tiles/pallas_call | solution.py:228
  (11 shorter events, 0.1 us)
Async XLA Ops:
  0.0 11.5 %copy-start = (s32[2,1,2,1]{2,3,1,0:T(1,128)S(1)}, s32[2,1,2,1]{2,3,1,0:T(1,128)}, u32[]{:S(2)}) copy-start(s32[2,1,2,1]{2,3,1,0:T(1,128)} %param.6) | copy-start | bytes 52
  2.0 24.2 %all-to-all-start = ((bf16[32,4,16,128]{3,2,1,0:T(8,128)(2,1)}), bf16[32,4,16,128]{3,2,1,0:T(8,128)(2,1)S(1)}, u32[]{:S(2)}, u32[]{:S(2)}) async-start(bf16[32,4,16,128]{3,2,1,0:T(8,128)(2,1)} %top_rows.1), calls=%async_computation | async-start | bytes 1048576 | tf_op jit(solution)/shard_map/all_to_all | solution.py:260
  13.2 22.8 %collective-permute-start = (bf16[608,128]{1,0:T(8,128)(2,1)S(1)}, bf16[608,128]{1,0:T(8,128)(2,1)S(1)}, u32[]{:S(2)}, u32[]{:S(2)}) collective-permute-start(bf16[608,128]{1,0:T(8,128)(2,1)S(1)} %get-tuple-element.12), channel_id=1, source_target_pairs={{0,2},{1,15},{16,18},{17,31},{32,34},{33,47},{48,50},{49,63},{64,6... | collective-permute-start | bytes 466952 | tf_op jit(solution)/shard_map/ppermute | solution.py:257
  16.6 19.5 %collective-permute-start.1 = (bf16[608,128]{1,0:T(8,128)(2,1)S(1)}, bf16[608,128]{1,0:T(8,128)(2,1)S(1)}, u32[]{:S(2)}, u32[]{:S(2)}) collective-permute-start(bf16[608,128]{1,0:T(8,128)(2,1)S(1)} %get-tuple-element.13), channel_id=1, source_target_pairs={{0,12},{1,5},{16,28},{17,21},{32,44},{33,37},{48,60},{49,53},{64,7... | collective-permute-start | bytes 466952 | tf_op jit(solution)/shard_map/ppermute | solution.py:258
  24.8 11.2 %collective-permute-start.2 = (bf16[608,128]{1,0:T(8,128)(2,1)S(1)}, bf16[608,128]{1,0:T(8,128)(2,1)S(1)}, u32[]{:S(2)}, u32[]{:S(2)}) collective-permute-start(bf16[608,128]{1,0:T(8,128)(2,1)S(1)} %get-tuple-element.14), channel_id=1, source_target_pairs={{0,6},{1,11},{16,22},{17,27},{32,38},{33,43},{48,54},{49,59},{64,7... | collective-permute-start | bytes 466952 | tf_op jit(solution)/shard_map/ppermute | solution.py:259
  26.9 23.6 %all-to-all-start.1 = ((bf16[16,32,128]{2,1,0:T(8,128)(2,1)}), bf16[16,32,128]{2,1,0:T(8,128)(2,1)S(1)}, u32[]{:S(2)}, u32[]{:S(2)}) async-start(bf16[16,32,128]{2,1,0:T(8,128)(2,1)} %broadcast_in_dim.4), calls=%async_computation.1 | async-start | bytes 262144 | tf_op jit(solution)/shard_map/all_to_all | solution.py:247
  36.1 8.9 %collective-permute-start.3 = (bf16[368,128]{1,0:T(8,128)(2,1)S(1)}, bf16[368,128]{1,0:T(8,128)(2,1)S(1)}, u32[]{:S(2)}, u32[]{:S(2)}) collective-permute-start(bf16[368,128]{1,0:T(8,128)(2,1)S(1)} %slice.55), channel_id=1, source_target_pairs={{0,14},{2,4},{6,8},{12,10},{1,3},{5,7},{11,9},{15,13},{16,30},{18,... | collective-permute-start | bytes 282632 | tf_op jit(solution)/shard_map/ppermute | solution.py:271
  51.9 42.1 %all-to-all-start.2 = ((bf16[32,192,128]{2,1,0:T(8,128)(2,1)}), bf16[32,192,128]{2,1,0:T(8,128)(2,1)S(1)}, u32[]{:S(2)}, u32[]{:S(2)}) async-start(bf16[32,192,128]{2,1,0:T(8,128)(2,1)} %broadcast_in_dim.5), calls=%async_computation.2 | async-start | bytes 3145728 | tf_op jit(solution)/shard_map/all_to_all | solution.py:247
  57.4 36.6 %collective-permute-start.4 = (bf16[128,128]{1,0:T(8,128)(2,1)S(1)}, bf16[128,128]{1,0:T(8,128)(2,1)S(1)}, u32[]{:S(2)}, u32[]{:S(2)}) collective-permute-start(bf16[128,128]{1,0:T(8,128)(2,1)S(1)} %slice_select_fusion.1.mine), channel_id=1, source_target_pairs={{0,1},{1,0},{2,3},{3,2},{4,5},{5,4},{6,7},{7,6},{8,9},{9,8},{10,11... | collective-permute-start | bytes 98312 | tf_op jit(solution)/shard_map/ppermute | solution.py:274

commit v6 on v5

--- a/solution.py
+++ b/solution.py
@@ -137,12 +137,16 @@
 
     @pl.when(step == 0)
     def _():
-        pairs = (
-            (inverses_hbm, inverses),
-            (left_hbm.at[:, 0, :, 0], left),
-            (right_hbm.at[:, 0, :, 0], right),
-        )
-        copies = fetch(pairs, arrived)
+        copies = [
+            pltpu.make_async_copy(inverses_hbm.at[k], inverses.at[k], arrived.at[k])
+            for k in range(2)
+        ]
+        tiles = [
+            pltpu.make_async_copy(left_hbm.at[:, 0, :, 0], left, arrived.at[2]),
+            pltpu.make_async_copy(right_hbm.at[:, 0, :, 0], right, arrived.at[3]),
+        ]
+        for copy in copies:
+            copy.start()
         ups[...] = jnp.concatenate([row_tile(0), row_tile(1), row_tile(10)], axis=1)
         for k in range(2):
             wide[:, 256 * k : 256 * k + 128] = row_tile(4 + k)
@@ -150,6 +154,9 @@
             upper[k, :, 128:] = row_tile(2 + k)
         copies[0].wait()
         lowers[:, 256:] = tn(inverses[0], row_tile(9)).astype(BF16)
+        for copy in tiles:
+            copy.start()
+        copies[1].wait()
         pivot = tn(inverses[1], row_tile(11)).astype(BF16)
         second[:, 128:256] = pivot
         second[:, 384:] = pivot
@@ -195,8 +202,8 @@
             result = -nn(tall[k], inner[256 * k : 256 * (k + 1)])
             for j in range(2):
                 change[k, j] = result[:, 256 * j : 256 * (j + 1)].astype(BF16)
-        copies[1].wait()
-        copies[2].wait()
+        for copy in tiles:
+            copy.wait()
 
     row = a * N_ROW + p
     col = b * N_COL + q
@@ -267,15 +274,18 @@
     by_middle = (q == 12) | (q == 5)
     is_head = (q < 2) | by_near | by_middle | (q == 6) | (q == 11)
     head = jnp.where(q < 2, own, jnp.where(by_near, near, jnp.where(by_middle, middle, far)))
+    block = scattered.reshape(128, 128)
+    sent = jnp.broadcast_to(jnp.pad(block, ((0, 64), (0, 0)))[None], (N_ROW, 192, 128))
+    sent, head = lax.optimization_barrier((sent, head))
     hops = [(line[k], line[k + 1]) for line in HOLDERS for k in range(0, 8, 2)]
     moved = lax.ppermute(head[MAIN:], "col", hops)
     piece = jnp.where(is_head, head[:MAIN], moved[:MAIN])
     mine = jnp.where(is_head, head[2 * MAIN :], moved[MAIN:])
     other = lax.ppermute(mine, "col", [(i, i ^ 1) for i in range(N_COL)])
 
-    block = jnp.concatenate([scattered.reshape(128, 128), corner], axis=0)
-    block, piece = lax.optimization_barrier((block, piece))
-    rows = to_all(block, "row", N_ROW).reshape(N_ROW, 12, 16, 128)
+    sent = sent.at[:, 128:].set(jnp.broadcast_to(corner[None], (N_ROW, 64, 128)))
+    sent, piece = lax.optimization_barrier((sent, piece))
+    rows = lax.all_to_all(sent, "row", 0, 0, tiled=True).reshape(N_ROW, 12, 16, 128)
     main = lax.all_gather(piece, "col")
     return update_tiles(place, ranks, left, right, main, mine, other, rows, pivot_inverses)
 

time: 102 us -> 101 us (level)
  waiting for transfers between devices: 8.31 us -> 6.81 us
    all_to_all x2 -> x1, starting transfers between devices: 14.6 us -> 9.15 us  [to_all(): return lax.all_to_all(sent, axis, 0, 0, tiled=True)]
    all_to_all x0 -> x1, starting transfers between devices: none -> 5.41 us  [per_device(): lax.all_to_all(sent, 'row', 0, 0, tiled=True).reshape(N_ROW, 12, 16, 128)]
    broadcast_in_dim x2 -> x1, local copies, waits for them, and re-layouts: 2.17 us -> 0.67 us  [to_all(): sent = jnp.broadcast_to(block[None], (size,) + block.shape)]
    broadcast_in_dim x0 -> x1, local copies, waits for them, and re-layouts: none -> 1.5 us  [per_device(): jnp.broadcast_to(jnp.pad(block, ((0, 64), (0, 0)))[None], (N_ROW, 192, 128))]
    all_to_all x2 -> x1, waiting for transfers between devices: 5.32 us -> 4.11 us  [to_all(): return lax.all_to_all(sent, axis, 0, 0, tiled=True)]
  transfers between devices with their start and end apart: 8 -> 8, of which waited for: 2 -> 2; matrix products, arithmetic and copies ran while one was open for 1% -> 2% of each run, Pallas kernels for 2% -> 2%
where the time goes in v6:
time: 101 us
  starting transfers between devices  46.1 us (46%)
  blocking collectives  33.4 us (33%)
  Pallas kernels  10.9 us (11%)
  waiting for transfers between devices  6.81 us (7%)
  local copies, waits for them, and re-layouts  3.11 us (3%)
    all_gather x1, blocking collectives, per_device(): main = lax.all_gather(piece, 'col')  33.4 us
    all_to_all x1, starting transfers between devices, per_device(): scattered = lax.all_to_all(top, 'row', 0, 0, tiled=True)[:2]  9.47 us
    all_to_all x1, starting transfers between devices, to_all(): return lax.all_to_all(sent, axis, 0, 0, tiled=True)  9.15 us
    ppermute x1, starting transfers between devices, per_device(): middle = lax.ppermute(middle, 'col', [(0, 12), (1, 5)])  8.23 us
    pallas_call x1, Pallas kernels, update_tiles(): pl.pallas_call(update_body, grid=(4,), out_shape=jax.ShapeDtypeStruct((2,...  7.21 us
    ppermute x1, starting transfers between devices, per_device(): moved = lax.ppermute(head[MAIN:], 'col', hops)  5.94 us
    all_to_all x1, starting transfers between devices, per_device(): lax.all_to_all(sent, 'row', 0, 0, tiled=True).reshape(N_ROW, 12, 16, 128)  5.41 us
    all_to_all x1, waiting for transfers between devices, to_all(): return lax.all_to_all(sent, axis, 0, 0, tiled=True)  4.11 us
  transfers between devices with their start and end apart: 8, of which 2 were waited for; matrix products, arithmetic and copies ran while one was open for 2% of the time, Pallas kernels for 2%

profile of v6, /device:TPU:2, one launch (start us, length us, event | category | flops | bytes accessed | tf_op | source)
XLA Modules:
  0.0 100.6 jit_solution(4785112265751193962)
XLA Ops:
  0.0 2.0 %top_rows.1 = bf16[32,4,16,128]{3,2,1,0:T(8,128)(2,1)} custom-call(s32[2,1,1,2]{3,2,1,0:T(1,128)} %bitcast.15, bf16[2,1,2,1,512,128]{5,4,3,2,1,0:T(8,128)(2,1)} %left_hbm.1, bf16[2,1,2,1,512,128]{5,4,3,2,1,0:T(8,128)(2,1)} %right_hbm.1), custom_call_target="tpu_custom_call" | custom-call | flops 1000000 | bytes 1048576 | tf_op jit(solution)/shard_map/top_rows/pallas_call | solution.py:78
  2.0 9.5 %all-to-all-start = ((bf16[32,4,16,128]{3,2,1,0:T(8,128)(2,1)}), bf16[32,4,16,128]{3,2,1,0:T(8,128)(2,1)S(1)}, u32[]{:S(2)}, u32[]{:S(2)}) async-start(bf16[32,4,16,128]{3,2,1,0:T(8,128)(2,1)} %top_rows.1), calls=%async_computation | async-start | bytes 1048576 | tf_op jit(solution)/shard_map/all_to_all | solution.py:267
  11.5 0.1 pad_add_fusion.place
  11.5 1.7 %messages.1 = (bf16[608,128]{1,0:T(8,128)(2,1)S(1)}, bf16[608,128]{1,0:T(8,128)(2,1)S(1)}, bf16[608,128]{1,0:T(8,128)(2,1)S(1)}, bf16[608,128]{1,0:T(8,128)(2,1)S(1)}) custom-call(s32[2]{0:T(128)S(1)} %pad_add_fusion.place, s32[2,1,1,2]{3,2,1,0:T(1,128)S(1)} %bitcast.16, bf16[2,1,2,1,512,128]{5,4,3,2,1,0:T(8,128)(2,1)} %left_hbm.1, ...), custom_call_target="tpu_custom_call" | custom-call | flops 1000000 | bytes 1048576 | tf_op jit(solution)/shard_map/messages/pallas_call | solution.py:115
  13.2 3.3 %collective-permute-start = (bf16[608,128]{1,0:T(8,128)(2,1)S(1)}, bf16[608,128]{1,0:T(8,128)(2,1)S(1)}, u32[]{:S(2)}, u32[]{:S(2)}) collective-permute-start(bf16[608,128]{1,0:T(8,128)(2,1)S(1)} %get-tuple-element.26), channel_id=1, source_target_pairs={{0,2},{1,15},{16,18},{17,31},{32,34},{33,47},{48,50},{49,63},{64,6... | collective-permute-start | bytes 466952 | tf_op jit(solution)/shard_map/ppermute | solution.py:264
  16.6 8.2 %collective-permute-start.1 = (bf16[608,128]{1,0:T(8,128)(2,1)S(1)}, bf16[608,128]{1,0:T(8,128)(2,1)S(1)}, u32[]{:S(2)}, u32[]{:S(2)}) collective-permute-start(bf16[608,128]{1,0:T(8,128)(2,1)S(1)} %get-tuple-element.27), channel_id=1, source_target_pairs={{0,12},{1,5},{16,28},{17,21},{32,44},{33,37},{48,60},{49,53},{64,7... | collective-permute-start | bytes 466952 | tf_op jit(solution)/shard_map/ppermute | solution.py:265
  24.8 1.3 %collective-permute-start.2 = (bf16[608,128]{1,0:T(8,128)(2,1)S(1)}, bf16[608,128]{1,0:T(8,128)(2,1)S(1)}, u32[]{:S(2)}, u32[]{:S(2)}) collective-permute-start(bf16[608,128]{1,0:T(8,128)(2,1)S(1)} %get-tuple-element.28), channel_id=1, source_target_pairs={{0,6},{1,11},{16,22},{17,27},{32,38},{33,43},{48,54},{49,59},{64,7... | collective-permute-start | bytes 466952 | tf_op jit(solution)/shard_map/ppermute | solution.py:266
  26.1 0.0 all-to-all-done
  26.2 0.7 broadcast_in_dim.7
  26.9 9.2 %all-to-all-start.1 = ((bf16[16,32,128]{2,1,0:T(8,128)(2,1)}), bf16[16,32,128]{2,1,0:T(8,128)(2,1)S(1)}, u32[]{:S(2)}, u32[]{:S(2)}) async-start(bf16[16,32,128]{2,1,0:T(8,128)(2,1)} %broadcast_in_dim.7), calls=%async_computation.1 | async-start | bytes 262144 | tf_op jit(solution)/shard_map/all_to_all | solution.py:254
  36.0 0.0 collective-permute-done
  36.0 0.0 collective-permute-done.1
  36.0 0.0 collective-permute-done.2
  36.1 1.5 %broadcast_in_dim.6 = bf16[32,192,128]{2,1,0:T(8,128)(2,1)} broadcast(bf16[192,128]{1,0:T(8,128)(2,1)S(1)} %pad.6), dimensions={1,2} | broadcast | bytes 1622016 | tf_op jit(solution)/shard_map/broadcast_in_dim | solution.py:278
  37.6 5.9 %collective-permute-start.3 = (bf16[368,128]{1,0:T(8,128)(2,1)S(1)}, bf16[368,128]{1,0:T(8,128)(2,1)S(1)}, u32[]{:S(2)}, u32[]{:S(2)}) collective-permute-start(bf16[368,128]{1,0:T(8,128)(2,1)S(1)} %slice.66), channel_id=1, source_target_pairs={{0,14},{2,4},{6,8},{12,10},{1,3},{5,7},{11,9},{15,13},{16,30},{18,... | collective-permute-start | bytes 282632 | tf_op jit(solution)/shard_map/ppermute | solution.py:281
  43.6 2.7 %collective-permute-done.3 = bf16[368,128]{1,0:T(8,128)(2,1)S(1)} collective-permute-done((bf16[368,128]{1,0:T(8,128)(2,1)S(1)}, bf16[368,128]{1,0:T(8,128)(2,1)S(1)}, u32[]{:S(2)}, u32[]{:S(2)}) %collective-permute-start.3) | collective-permute-done | bytes 94240 | tf_op jit(solution)/shard_map/ppermute | solution.py:281
  46.3 4.1 %all-to-all-done.1 = bf16[16,32,128]{2,1,0:T(8,128)(2,1)S(1)} async-done(((bf16[16,32,128]{2,1,0:T(8,128)(2,1)}), bf16[16,32,128]{2,1,0:T(8,128)(2,1)S(1)}, u32[]{:S(2)}, u32[]{:S(2)}) %all-to-all-start.1) | async-done | bytes 131104 | tf_op jit(solution)/shard_map/all_to_all | solution.py:254
  50.4 0.9 broadcast_dynamic-update-slice_fusion
  51.3 5.4 %all-to-all-start.2 = ((bf16[32,192,128]{2,1,0:T(8,128)(2,1)}), bf16[32,192,128]{2,1,0:T(8,128)(2,1)S(1)}, u32[]{:S(2)}, u32[]{:S(2)}) async-start(bf16[32,192,128]{2,1,0:T(8,128)(2,1)} %broadcast_dynamic-update-slice_fusion), calls=%async_computation.2 | async-start | bytes 3145728 | tf_op jit(solution)/shard_map/all_to_all | solution.py:288
  56.8 3.3 %collective-permute-start.4 = (bf16[128,128]{1,0:T(8,128)(2,1)S(1)}, bf16[128,128]{1,0:T(8,128)(2,1)S(1)}, u32[]{:S(2)}, u32[]{:S(2)}) collective-permute-start(bf16[128,128]{1,0:T(8,128)(2,1)S(1)} %slice_select_fusion.1.mine), channel_id=1, source_target_pairs={{0,1},{1,0},{2,3},{3,2},{4,5},{5,4},{6,7},{7,6},{8,9},{9,8},{10,11... | collective-permute-start | bytes 98312 | tf_op jit(solution)/shard_map/ppermute | solution.py:284
  60.0 33.4 %all-gather = bf16[3840,128]{1,0:T(8,128)(2,1)S(1)} all-gather(bf16[240,128]{1,0:T(8,128)(2,1)S(1)} %slice_select_fusion), channel_id=2, replica_groups=mesh['row'=32,'col'=16] {'col'}, dimensions={0}, use_global_device_ids=true | all-gather | bytes 1044480 | tf_op jit(solution)/shard_map/all_gather | solution.py:289
  93.4 0.0 collective-permute-done.4.other
  93.4 0.0 all-to-all-done.2
  93.4 7.2 %update_tiles.1 = bf16[2,1,2,1,512,512]{5,4,3,2,1,0:T(8,128)(2,1)} custom-call(s32[2]{0:T(128)S(1)} %pad_add_fusion.place, s32[2,1,1,2]{3,2,1,0:T(1,128)S(1)} %bitcast.17, bf16[2,1,2,1,512,128]{5,4,3,2,1,0:T(8,128)(2,1)} %left_hbm.1, bf16[2,1,2,1,512,128]{5,4,3,2,1,0:T(8,128)(2,1)} %right_hbm.1, bf16[2,512,512]{2,1,0:T(8,128)(2,1)} %inverses_hbm.1, ...), custom_call_target="tpu_custom_call" | custom-call | flops 2500000000 | bytes 8388608 | tf_op jit(solution)/shard_map/update_tiles/pallas_call | solution.py:235
  (12 shorter events, 0.1 us)
Async XLA Ops:
  0.0 11.5 %copy-start = (s32[2,1,2,1]{2,3,1,0:T(1,128)S(1)}, s32[2,1,2,1]{2,3,1,0:T(1,128)}, u32[]{:S(2)}) copy-start(s32[2,1,2,1]{2,3,1,0:T(1,128)} %param.8) | copy-start | bytes 52
  2.0 24.2 %all-to-all-start = ((bf16[32,4,16,128]{3,2,1,0:T(8,128)(2,1)}), bf16[32,4,16,128]{3,2,1,0:T(8,128)(2,1)S(1)}, u32[]{:S(2)}, u32[]{:S(2)}) async-start(bf16[32,4,16,128]{3,2,1,0:T(8,128)(2,1)} %top_rows.1), calls=%async_computation | async-start | bytes 1048576 | tf_op jit(solution)/shard_map/all_to_all | solution.py:267
  13.2 22.8 %collective-permute-start = (bf16[608,128]{1,0:T(8,128)(2,1)S(1)}, bf16[608,128]{1,0:T(8,128)(2,1)S(1)}, u32[]{:S(2)}, u32[]{:S(2)}) collective-permute-start(bf16[608,128]{1,0:T(8,128)(2,1)S(1)} %get-tuple-element.26), channel_id=1, source_target_pairs={{0,2},{1,15},{16,18},{17,31},{32,34},{33,47},{48,50},{49,63},{64,6... | collective-permute-start | bytes 466952 | tf_op jit(solution)/shard_map/ppermute | solution.py:264
  16.6 19.4 %collective-permute-start.1 = (bf16[608,128]{1,0:T(8,128)(2,1)S(1)}, bf16[608,128]{1,0:T(8,128)(2,1)S(1)}, u32[]{:S(2)}, u32[]{:S(2)}) collective-permute-start(bf16[608,128]{1,0:T(8,128)(2,1)S(1)} %get-tuple-element.27), channel_id=1, source_target_pairs={{0,12},{1,5},{16,28},{17,21},{32,44},{33,37},{48,60},{49,53},{64,7... | collective-permute-start | bytes 466952 | tf_op jit(solution)/shard_map/ppermute | solution.py:265
  24.8 11.2 %collective-permute-start.2 = (bf16[608,128]{1,0:T(8,128)(2,1)S(1)}, bf16[608,128]{1,0:T(8,128)(2,1)S(1)}, u32[]{:S(2)}, u32[]{:S(2)}) collective-permute-start(bf16[608,128]{1,0:T(8,128)(2,1)S(1)} %get-tuple-element.28), channel_id=1, source_target_pairs={{0,6},{1,11},{16,22},{17,27},{32,38},{33,43},{48,54},{49,59},{64,7... | collective-permute-start | bytes 466952 | tf_op jit(solution)/shard_map/ppermute | solution.py:266
  26.9 23.6 %all-to-all-start.1 = ((bf16[16,32,128]{2,1,0:T(8,128)(2,1)}), bf16[16,32,128]{2,1,0:T(8,128)(2,1)S(1)}, u32[]{:S(2)}, u32[]{:S(2)}) async-start(bf16[16,32,128]{2,1,0:T(8,128)(2,1)} %broadcast_in_dim.7), calls=%async_computation.1 | async-start | bytes 262144 | tf_op jit(solution)/shard_map/all_to_all | solution.py:254
  37.6 8.7 %collective-permute-start.3 = (bf16[368,128]{1,0:T(8,128)(2,1)S(1)}, bf16[368,128]{1,0:T(8,128)(2,1)S(1)}, u32[]{:S(2)}, u32[]{:S(2)}) collective-permute-start(bf16[368,128]{1,0:T(8,128)(2,1)S(1)} %slice.66), channel_id=1, source_target_pairs={{0,14},{2,4},{6,8},{12,10},{1,3},{5,7},{11,9},{15,13},{16,30},{18,... | collective-permute-start | bytes 282632 | tf_op jit(solution)/shard_map/ppermute | solution.py:281
  51.3 42.1 %all-to-all-start.2 = ((bf16[32,192,128]{2,1,0:T(8,128)(2,1)}), bf16[32,192,128]{2,1,0:T(8,128)(2,1)S(1)}, u32[]{:S(2)}, u32[]{:S(2)}) async-start(bf16[32,192,128]{2,1,0:T(8,128)(2,1)} %broadcast_dynamic-update-slice_fusion), calls=%async_computation.2 | async-start | bytes 3145728 | tf_op jit(solution)/shard_map/all_to_all | solution.py:288
  56.8 36.6 %collective-permute-start.4 = (bf16[128,128]{1,0:T(8,128)(2,1)S(1)}, bf16[128,128]{1,0:T(8,128)(2,1)S(1)}, u32[]{:S(2)}, u32[]{:S(2)}) collective-permute-start(bf16[128,128]{1,0:T(8,128)(2,1)S(1)} %slice_select_fusion.1.mine), channel_id=1, source_target_pairs={{0,1},{1,0},{2,3},{3,2},{4,5},{5,4},{6,7},{7,6},{8,9},{9,8},{10,11... | collective-permute-start | bytes 98312 | tf_op jit(solution)/shard_map/ppermute | solution.py:284

commit v7 on v6

--- a/solution.py
+++ b/solution.py
@@ -62,26 +62,32 @@
     return copies
 
 
-def top_body(ranks_hbm, left, right, top, ranks, tiles, arrived):
+def top_body(ranks_hbm, left, right, top, panel, ranks, tiles, arrived):
     pairs = [(ranks_hbm, ranks)]
     for t in range(4):
         source = (left, right)[t // 2]
         pairs.append((source.at[0, 0, t % 2, 0], tiles.at[t]))
+    pairs += [(left.at[:, 0, 0, 0], panel.at[0]), (right.at[:, 0, 0, 0], panel.at[1])]
     copies = fetch(pairs, arrived)
     copies[0].wait()
     for t in range(4):
         copies[1 + t].wait()
         top[:, t] = mask_rank(tiles[t], ranks[0, 0, 0, t % 2]).reshape(N_ROW, 16, 128)
+    for copy in copies[5:]:
+        copy.wait()
 
 
 def top_rows(ranks, left, right):
     return pl.pallas_call(
         top_body,
-        out_shape=jax.ShapeDtypeStruct((N_ROW, 4, 16, 128), BF16),
+        out_shape=(
+            jax.ShapeDtypeStruct((N_ROW, 4, 16, 128), BF16),
+            jax.ShapeDtypeStruct((2, 2, 512, 128), BF16),
+        ),
         in_specs=[HBM] * 3,
-        out_specs=VMEM,
+        out_specs=[VMEM] * 2,
         scratch_shapes=[pltpu.SMEM((2, 1, 1, 2), jnp.int32)]
-        + [pltpu.VMEM((4, 512, 128), BF16), pltpu.SemaphoreType.DMA((5,))],
+        + [pltpu.VMEM((4, 512, 128), BF16), pltpu.SemaphoreType.DMA((7,))],
         compiler_params=params(),
         cost_estimate=cost(10**6, 2**20),
         name="top_rows",
@@ -89,12 +95,9 @@
 
 
 def messages_body(
-    place, ranks, left, right, own, near, middle, far, left_col, right_col, arrived
+    place, ranks, panel, own, near, middle, far
 ):
-    pairs = ((left.at[:, 0, 0, 0], left_col), (right.at[:, 0, 0, 0], right_col))
-    for copy in fetch(pairs, arrived):
-        copy.wait()
-    tiles = [mask_rank(ref[a], ranks[a, 0, 0, 0]) for ref in (left_col, right_col) for a in range(2)]
+    tiles = [mask_rank(panel[k, a], ranks[a, 0, 0, 0]) for k in range(2) for a in range(2)]
     at_zero = place[1] == 0
     chosen = (
         tiles[0],
@@ -110,18 +113,17 @@
             message[2 * MAIN + REST * k : 2 * MAIN + REST * (k + 1)] = rest
 
 
-def messages(place, ranks, left, right):
+def messages(place, ranks, panel):
     message = jax.ShapeDtypeStruct((2 * MAIN + 8 * REST, 128), BF16)
     return pl.pallas_call(
         messages_body,
         out_shape=(message,) * 4,
-        in_specs=[SMEM, SMEM, HBM, HBM],
+        in_specs=[SMEM, SMEM, VMEM],
         out_specs=[VMEM] * 4,
-        scratch_shapes=[pltpu.VMEM((2, 512, 128), BF16)] * 2 + [pltpu.SemaphoreType.DMA((2,))],
         compiler_params=params(),
         cost_estimate=cost(10**6, 2**20),
         name="messages",
-    )(place, ranks, *in_hbm(left, right))
+    )(place, ranks, panel)
 
 
 def update_body(
@@ -259,8 +261,8 @@
     q = lax.axis_index("col")
     place = jnp.stack([p, q]).astype(jnp.int32)
     ranks = ranks.reshape(2, 1, 1, 2)
-    top = top_rows(ranks, left, right)
-    own, near, middle, far = messages(place, ranks, left, right)
+    top, panel = top_rows(ranks, left, right)
+    own, near, middle, far = messages(place, ranks, panel)
     near = lax.ppermute(near, "col", [(0, 2), (1, 15)])
     middle = lax.ppermute(middle, "col", [(0, 12), (1, 5)])
     far = lax.ppermute(far, "col", [(0, 6), (1, 11)])

time: 101 us -> 101 us (level)
    all_to_all x1, starting transfers between devices: 9.15 us -> 10.2 us  [to_all(): return lax.all_to_all(sent, axis, 0, 0, tiled=True)]
    pallas_call x1, Pallas kernels: 1.68 us -> 0.64 us  [messages(): pl.pallas_call(messages_body, out_shape=(message,) * 4, in_specs=[SMEM, S...]
  transfers between devices with their start and end apart: 8 -> 8, of which waited for: 2 -> 2; matrix products, arithmetic and copies ran while one was open for 2% -> 2% of each run, Pallas kernels for 2% -> 1%
where the time goes in v7:
time: 101 us
  starting transfers between devices  46.9 us (46%)
  blocking collectives  33.6 us (33%)
  Pallas kernels  10 us (10%)
  waiting for transfers between devices  6.81 us (7%)
  local copies, waits for them, and re-layouts  3.11 us (3%)
    all_gather x1, blocking collectives, per_device(): main = lax.all_gather(piece, 'col')  33.6 us
    all_to_all x1, starting transfers between devices, to_all(): return lax.all_to_all(sent, axis, 0, 0, tiled=True)  10.2 us
    all_to_all x1, starting transfers between devices, per_device(): scattered = lax.all_to_all(top, 'row', 0, 0, tiled=True)[:2]  9.47 us
    ppermute x1, starting transfers between devices, per_device(): middle = lax.ppermute(middle, 'col', [(0, 12), (1, 5)])  8.23 us
    pallas_call x1, Pallas kernels, update_tiles(): pl.pallas_call(update_body, grid=(4,), out_shape=jax.ShapeDtypeStruct((2,...  7.21 us
    ppermute x1, starting transfers between devices, per_device(): moved = lax.ppermute(head[MAIN:], 'col', hops)  5.94 us
    all_to_all x1, starting transfers between devices, per_device(): lax.all_to_all(sent, 'row', 0, 0, tiled=True).reshape(N_ROW, 12, 16, 128)  5.41 us
    all_to_all x1, waiting for transfers between devices, to_all(): return lax.all_to_all(sent, axis, 0, 0, tiled=True)  4.11 us
  transfers between devices with their start and end apart: 8, of which 2 were waited for; matrix products, arithmetic and copies ran while one was open for 2% of the time, Pallas kernels for 1%

profile of v7, /device:TPU:2, one launch (start us, length us, event | category | flops | bytes accessed | tf_op | source)
XLA Modules:
  0.0 100.8 jit_solution(15244380237254270109)
XLA Ops:
  0.0 2.2 %top_rows.1 = (bf16[32,4,16,128]{3,2,1,0:T(8,128)(2,1)}, bf16[2,2,512,128]{3,2,1,0:T(8,128)(2,1)S(1)}) custom-call(s32[2,1,1,2]{3,2,1,0:T(1,128)} %bitcast.15, bf16[2,1,2,1,512,128]{5,4,3,2,1,0:T(8,128)(2,1)} %left_hbm.1, bf16[2,1,2,1,512,128]{5,4,3,2,1,0:T(8,128)(2,1)} %right_hbm.1), custom_call_target="tpu_custom_call" | custom-call | flops 1000000 | bytes 1048576 | tf_op jit(solution)/shard_map/top_rows/pallas_call | solution.py:81
  2.2 9.5 %all-to-all-start = ((bf16[32,4,16,128]{3,2,1,0:T(8,128)(2,1)}), bf16[32,4,16,128]{3,2,1,0:T(8,128)(2,1)S(1)}, u32[]{:S(2)}, u32[]{:S(2)}) async-start(bf16[32,4,16,128]{3,2,1,0:T(8,128)(2,1)} %get-tuple-element.27), calls=%async_computation | async-start | bytes 1048576 | tf_op jit(solution)/shard_map/all_to_all | solution.py:269
  11.6 0.1 pad_add_fusion.place
  11.7 0.6 messages.1
  12.4 3.3 %collective-permute-start = (bf16[608,128]{1,0:T(8,128)(2,1)S(1)}, bf16[608,128]{1,0:T(8,128)(2,1)S(1)}, u32[]{:S(2)}, u32[]{:S(2)}) collective-permute-start(bf16[608,128]{1,0:T(8,128)(2,1)S(1)} %get-tuple-element.30), channel_id=1, source_target_pairs={{0,2},{1,15},{16,18},{17,31},{32,34},{33,47},{48,50},{49,63},{64,6... | collective-permute-start | bytes 466952 | tf_op jit(solution)/shard_map/ppermute | solution.py:266
  15.7 8.2 %collective-permute-start.1 = (bf16[608,128]{1,0:T(8,128)(2,1)S(1)}, bf16[608,128]{1,0:T(8,128)(2,1)S(1)}, u32[]{:S(2)}, u32[]{:S(2)}) collective-permute-start(bf16[608,128]{1,0:T(8,128)(2,1)S(1)} %get-tuple-element.31), channel_id=1, source_target_pairs={{0,12},{1,5},{16,28},{17,21},{32,44},{33,37},{48,60},{49,53},{64,7... | collective-permute-start | bytes 466952 | tf_op jit(solution)/shard_map/ppermute | solution.py:267
  24.0 1.3 %collective-permute-start.2 = (bf16[608,128]{1,0:T(8,128)(2,1)S(1)}, bf16[608,128]{1,0:T(8,128)(2,1)S(1)}, u32[]{:S(2)}, u32[]{:S(2)}) collective-permute-start(bf16[608,128]{1,0:T(8,128)(2,1)S(1)} %get-tuple-element.32), channel_id=1, source_target_pairs={{0,6},{1,11},{16,22},{17,27},{32,38},{33,43},{48,54},{49,59},{64,7... | collective-permute-start | bytes 466952 | tf_op jit(solution)/shard_map/ppermute | solution.py:268
  25.3 0.0 all-to-all-done
  25.3 0.7 broadcast_in_dim.7
  26.0 10.2 %all-to-all-start.1 = ((bf16[16,32,128]{2,1,0:T(8,128)(2,1)}), bf16[16,32,128]{2,1,0:T(8,128)(2,1)S(1)}, u32[]{:S(2)}, u32[]{:S(2)}) async-start(bf16[16,32,128]{2,1,0:T(8,128)(2,1)} %broadcast_in_dim.7), calls=%async_computation.1 | async-start | bytes 262144 | tf_op jit(solution)/shard_map/all_to_all | solution.py:256
  36.2 0.0 collective-permute-done
  36.2 0.0 collective-permute-done.1
  36.2 0.0 collective-permute-done.2
  36.3 1.5 %broadcast_in_dim.6 = bf16[32,192,128]{2,1,0:T(8,128)(2,1)} broadcast(bf16[192,128]{1,0:T(8,128)(2,1)S(1)} %pad.6), dimensions={1,2} | broadcast | bytes 1622016 | tf_op jit(solution)/shard_map/broadcast_in_dim | solution.py:280
  37.8 5.9 %collective-permute-start.3 = (bf16[368,128]{1,0:T(8,128)(2,1)S(1)}, bf16[368,128]{1,0:T(8,128)(2,1)S(1)}, u32[]{:S(2)}, u32[]{:S(2)}) collective-permute-start(bf16[368,128]{1,0:T(8,128)(2,1)S(1)} %slice.66), channel_id=1, source_target_pairs={{0,14},{2,4},{6,8},{12,10},{1,3},{5,7},{11,9},{15,13},{16,30},{18,... | collective-permute-start | bytes 282632 | tf_op jit(solution)/shard_map/ppermute | solution.py:283
  43.8 2.7 %collective-permute-done.3 = bf16[368,128]{1,0:T(8,128)(2,1)S(1)} collective-permute-done((bf16[368,128]{1,0:T(8,128)(2,1)S(1)}, bf16[368,128]{1,0:T(8,128)(2,1)S(1)}, u32[]{:S(2)}, u32[]{:S(2)}) %collective-permute-start.3) | collective-permute-done | bytes 94240 | tf_op jit(solution)/shard_map/ppermute | solution.py:283
  46.5 4.1 %all-to-all-done.1 = bf16[16,32,128]{2,1,0:T(8,128)(2,1)S(1)} async-done(((bf16[16,32,128]{2,1,0:T(8,128)(2,1)}), bf16[16,32,128]{2,1,0:T(8,128)(2,1)S(1)}, u32[]{:S(2)}, u32[]{:S(2)}) %all-to-all-start.1) | async-done | bytes 131104 | tf_op jit(solution)/shard_map/all_to_all | solution.py:256
  50.6 0.9 broadcast_dynamic-update-slice_fusion
  51.5 5.4 %all-to-all-start.2 = ((bf16[32,192,128]{2,1,0:T(8,128)(2,1)}), bf16[32,192,128]{2,1,0:T(8,128)(2,1)S(1)}, u32[]{:S(2)}, u32[]{:S(2)}) async-start(bf16[32,192,128]{2,1,0:T(8,128)(2,1)} %broadcast_dynamic-update-slice_fusion), calls=%async_computation.2 | async-start | bytes 3145728 | tf_op jit(solution)/shard_map/all_to_all | solution.py:290
  57.0 3.1 %collective-permute-start.4 = (bf16[128,128]{1,0:T(8,128)(2,1)S(1)}, bf16[128,128]{1,0:T(8,128)(2,1)S(1)}, u32[]{:S(2)}, u32[]{:S(2)}) collective-permute-start(bf16[128,128]{1,0:T(8,128)(2,1)S(1)} %slice_select_fusion.1.mine), channel_id=1, source_target_pairs={{0,1},{1,0},{2,3},{3,2},{4,5},{5,4},{6,7},{7,6},{8,9},{9,8},{10,11... | collective-permute-start | bytes 98312 | tf_op jit(solution)/shard_map/ppermute | solution.py:286
  60.0 33.6 %all-gather = bf16[3840,128]{1,0:T(8,128)(2,1)S(1)} all-gather(bf16[240,128]{1,0:T(8,128)(2,1)S(1)} %slice_select_fusion), channel_id=2, replica_groups=mesh['row'=32,'col'=16] {'col'}, dimensions={0}, use_global_device_ids=true | all-gather | bytes 1044480 | tf_op jit(solution)/shard_map/all_gather | solution.py:291
  93.6 0.0 collective-permute-done.4.other
  93.6 0.0 all-to-all-done.2
  93.6 7.2 %update_tiles.1 = bf16[2,1,2,1,512,512]{5,4,3,2,1,0:T(8,128)(2,1)} custom-call(s32[2]{0:T(128)S(1)} %pad_add_fusion.place, s32[2,1,1,2]{3,2,1,0:T(1,128)S(1)} %bitcast.17, bf16[2,1,2,1,512,128]{5,4,3,2,1,0:T(8,128)(2,1)} %left_hbm.1, bf16[2,1,2,1,512,128]{5,4,3,2,1,0:T(8,128)(2,1)} %right_hbm.1, bf16[2,512,512]{2,1,0:T(8,128)(2,1)} %inverses_hbm.1, ...), custom_call_target="tpu_custom_call" | custom-call | flops 2500000000 | bytes 8388608 | tf_op jit(solution)/shard_map/update_tiles/pallas_call | solution.py:237
  (12 shorter events, 0.1 us)
Async XLA Ops:
  0.0 11.7 %copy-start = (s32[2,1,2,1]{2,3,1,0:T(1,128)S(1)}, s32[2,1,2,1]{2,3,1,0:T(1,128)}, u32[]{:S(2)}) copy-start(s32[2,1,2,1]{2,3,1,0:T(1,128)} %param.8) | copy-start | bytes 52
  2.2 23.1 %all-to-all-start = ((bf16[32,4,16,128]{3,2,1,0:T(8,128)(2,1)}), bf16[32,4,16,128]{3,2,1,0:T(8,128)(2,1)S(1)}, u32[]{:S(2)}, u32[]{:S(2)}) async-start(bf16[32,4,16,128]{3,2,1,0:T(8,128)(2,1)} %get-tuple-element.27), calls=%async_computation | async-start | bytes 1048576 | tf_op jit(solution)/shard_map/all_to_all | solution.py:269
  12.4 23.8 %collective-permute-start = (bf16[608,128]{1,0:T(8,128)(2,1)S(1)}, bf16[608,128]{1,0:T(8,128)(2,1)S(1)}, u32[]{:S(2)}, u32[]{:S(2)}) collective-permute-start(bf16[608,128]{1,0:T(8,128)(2,1)S(1)} %get-tuple-element.30), channel_id=1, source_target_pairs={{0,2},{1,15},{16,18},{17,31},{32,34},{33,47},{48,50},{49,63},{64,6... | collective-permute-start | bytes 466952 | tf_op jit(solution)/shard_map/ppermute | solution.py:266
  15.7 20.5 %collective-permute-start.1 = (bf16[608,128]{1,0:T(8,128)(2,1)S(1)}, bf16[608,128]{1,0:T(8,128)(2,1)S(1)}, u32[]{:S(2)}, u32[]{:S(2)}) collective-permute-start(bf16[608,128]{1,0:T(8,128)(2,1)S(1)} %get-tuple-element.31), channel_id=1, source_target_pairs={{0,12},{1,5},{16,28},{17,21},{32,44},{33,37},{48,60},{49,53},{64,7... | collective-permute-start | bytes 466952 | tf_op jit(solution)/shard_map/ppermute | solution.py:267
  24.0 12.3 %collective-permute-start.2 = (bf16[608,128]{1,0:T(8,128)(2,1)S(1)}, bf16[608,128]{1,0:T(8,128)(2,1)S(1)}, u32[]{:S(2)}, u32[]{:S(2)}) collective-permute-start(bf16[608,128]{1,0:T(8,128)(2,1)S(1)} %get-tuple-element.32), channel_id=1, source_target_pairs={{0,6},{1,11},{16,22},{17,27},{32,38},{33,43},{48,54},{49,59},{64,7... | collective-permute-start | bytes 466952 | tf_op jit(solution)/shard_map/ppermute | solution.py:268
  26.0 24.6 %all-to-all-start.1 = ((bf16[16,32,128]{2,1,0:T(8,128)(2,1)}), bf16[16,32,128]{2,1,0:T(8,128)(2,1)S(1)}, u32[]{:S(2)}, u32[]{:S(2)}) async-start(bf16[16,32,128]{2,1,0:T(8,128)(2,1)} %broadcast_in_dim.7), calls=%async_computation.1 | async-start | bytes 262144 | tf_op jit(solution)/shard_map/all_to_all | solution.py:256
  37.8 8.7 %collective-permute-start.3 = (bf16[368,128]{1,0:T(8,128)(2,1)S(1)}, bf16[368,128]{1,0:T(8,128)(2,1)S(1)}, u32[]{:S(2)}, u32[]{:S(2)}) collective-permute-start(bf16[368,128]{1,0:T(8,128)(2,1)S(1)} %slice.66), channel_id=1, source_target_pairs={{0,14},{2,4},{6,8},{12,10},{1,3},{5,7},{11,9},{15,13},{16,30},{18,... | collective-permute-start | bytes 282632 | tf_op jit(solution)/shard_map/ppermute | solution.py:283
  51.5 42.1 %all-to-all-start.2 = ((bf16[32,192,128]{2,1,0:T(8,128)(2,1)}), bf16[32,192,128]{2,1,0:T(8,128)(2,1)S(1)}, u32[]{:S(2)}, u32[]{:S(2)}) async-start(bf16[32,192,128]{2,1,0:T(8,128)(2,1)} %broadcast_dynamic-update-slice_fusion), calls=%async_computation.2 | async-start | bytes 3145728 | tf_op jit(solution)/shard_map/all_to_all | solution.py:290
  57.0 36.6 %collective-permute-start.4 = (bf16[128,128]{1,0:T(8,128)(2,1)S(1)}, bf16[128,128]{1,0:T(8,128)(2,1)S(1)}, u32[]{:S(2)}, u32[]{:S(2)}) collective-permute-start(bf16[128,128]{1,0:T(8,128)(2,1)S(1)} %slice_select_fusion.1.mine), channel_id=1, source_target_pairs={{0,1},{1,0},{2,3},{3,2},{4,5},{5,4},{6,7},{7,6},{8,9},{9,8},{10,11... | collective-permute-start | bytes 98312 | tf_op jit(solution)/shard_map/ppermute | solution.py:286
